TPU v7x, 512 devices: a whole 4x4x16 slice. The times are simulated.
512 devices in a mesh: row: 32 (over x, y, core), col: 16 (over z).
Axes of the slice: x: 4, y: 4, z: 16, core: 2. Of those that a mesh axis runs over, the one named last changes fastest.
Arguments:
- user_embed: bfloat16 [16384, 256], P('row')
- item_embed: bfloat16 [16384, 256], P('col')
- positive: int32 [16384], P('row'), may hold values from 0 to 16383
- user_count: int32 [16384], P('row'), may hold values from 1 to 999
- item_count: int32 [16384], P('col'), may hold values from 1 to 999
Outputs:
- user_grad: float32 [16384, 256], P('row')
- item_grad: float32 [16384, 256], P('col')
- mean_loss: float32 [], replicated
All inputs are finite; a program needn't handle non-finite values.
Results may differ from a plain program's by a relative error of at most 0.0019.
Values sent between devices are 32-bit elements; how exact they have to be, the bound alone decides.
A program may use at most 64 MiB of HBM per device.

v0:
```python
import jax
import jax.numpy as jnp
from jax import lax
from jax.sharding import PartitionSpec as P


def joined(array, axis, combine):
    everything = jax.tree.map(lambda part: lax.all_gather(part, axis), array)
    first = jax.tree.map(lambda part: part[0], everything)

    def lap(k, so_far):
        return combine(so_far, jax.tree.map(lambda part: part[k], everything))

    return lax.fori_loop(1, lax.axis_size(axis), lap, first)


def pair_merge(max_one, sum_one, max_two, sum_two):
    top = jnp.maximum(max_one, max_two)
    return (top, sum_one * jnp.exp(max_one - top) + sum_two * jnp.exp(max_two - top))


def user_combine(first, second):
    top, total = pair_merge(first[0], first[1], second[0], second[1])
    return (top, total, first[2] + second[2], first[3] + second[3])


def item_combine(first, second):
    top, total = pair_merge(first[0], first[1], second[0], second[1])
    return (top, total, first[2] + second[2])


def per_device(user_embed, item_embed, positive, user_count, item_count):
    rows_here = user_embed.shape[0]
    cols_here = item_embed.shape[0]
    width = user_embed.shape[1]
    block_rows = min(512, rows_here)
    count_blocks = rows_here // block_rows
    col_offset = lax.axis_index("col") * cols_here
    log_item = jnp.log(item_count.astype(jnp.float32))
    log_user = jnp.log(user_count.astype(jnp.float32))
    columns = lax.iota(jnp.int32, cols_here)
    user_blocks = user_embed.reshape(count_blocks, block_rows, width)
    log_blocks = log_user.reshape(count_blocks, block_rows)
    pos_blocks = (positive - col_offset).reshape(count_blocks, block_rows)

    def scores_of(user_block):
        prod = lax.dot_general(
            user_block, item_embed, (((1,), (1,)), ((), ())), preferred_element_type=jnp.float32
        )
        return prod * 2.0

    def first(carry, inputs):
        col_max, col_sum, pos_hits = carry
        user_block, user_log, pos_block = inputs
        scores = scores_of(user_block)
        shifted = scores - log_item[None, :]
        row_max = jnp.max(shifted, axis=1)
        row_sum = jnp.sum(jnp.exp(shifted - row_max[:, None]), axis=1)
        matches = pos_block[:, None] == columns[None, :]
        z_shift = jnp.sum(jnp.where(matches, shifted, 0.0), axis=1)
        z_raw = jnp.sum(jnp.where(matches, scores, 0.0), axis=1)
        col_term = scores - user_log[:, None]
        new_max = jnp.maximum(col_max, jnp.max(col_term, axis=0))
        col_sum = col_sum * jnp.exp(col_max - new_max) + jnp.sum(
            jnp.exp(col_term - new_max[None, :]), axis=0
        )
        pos_hits = pos_hits + jnp.sum(matches.astype(jnp.float32), axis=0)
        return ((new_max, col_sum, pos_hits), (row_max, row_sum, z_shift, z_raw))

    start = (
        jnp.full((cols_here,), -1e30, jnp.float32),
        jnp.zeros((cols_here,), jnp.float32),
        jnp.zeros((cols_here,), jnp.float32),
    )
    (col_max, col_sum, pos_hits), row_stats = lax.scan(
        first, start, (user_blocks, log_blocks, pos_blocks)
    )
    row_max, row_sum, z_shift, z_raw = [piece.reshape(rows_here) for piece in row_stats]
    row_max, row_sum, z_shift, z_raw = joined(
        (row_max, row_sum, z_shift, z_raw), "col", user_combine
    )
    col_max, col_sum, pos_hits = joined((col_max, col_sum, pos_hits), "row", item_combine)
    row_lse = row_max + jnp.log(row_sum)
    col_lse = col_max + jnp.log(col_sum)
    user_terms = jnp.sum(row_lse - z_shift - z_raw + log_user)
    item_terms = jnp.sum(pos_hits * col_lse)
    local_loss = user_terms / lax.axis_size("col") + item_terms / lax.axis_size("row")
    mean_loss = lax.psum(local_loss, ("row", "col")) / (rows_here * lax.axis_size("row"))

    def second(item_acc, inputs):
        user_block, user_log, pos_block, lse_block = inputs
        scores = scores_of(user_block)
        matches = (pos_block[:, None] == columns[None, :]).astype(jnp.float32)
        row_part = jnp.exp(scores - log_item[None, :] - lse_block[:, None])
        col_part = pos_hits[None, :] * jnp.exp(scores - user_log[:, None] - col_lse[None, :])
        coupling = (row_part + col_part - 2.0 * matches).astype(jnp.bfloat16)
        user_part = jnp.dot(coupling, item_embed, preferred_element_type=jnp.float32) * 2.0
        item_part = (
            lax.dot_general(
                coupling, user_block, (((0,), (0,)), ((), ())), preferred_element_type=jnp.float32
            )
            * 2.0
        )
        return (item_acc + item_part, user_part)

    lse_blocks = row_lse.reshape(count_blocks, block_rows)
    item_acc, user_parts = lax.scan(
        second,
        jnp.zeros((cols_here, width), jnp.float32),
        (user_blocks, log_blocks, pos_blocks, lse_blocks),
    )
    user_grad = lax.psum(user_parts.reshape(rows_here, width), "col")
    item_grad = lax.psum(item_acc, "row")
    return (user_grad, item_grad, mean_loss)


def solution(mesh):
    in_specs = (P("row", None), P("col", None), P("row"), P("row"), P("col"))
    out_specs = (P("row", None), P("col", None), P())
    return jax.shard_map(
        per_device, mesh=mesh, in_specs=in_specs, out_specs=out_specs, check_vma=False
    )
```

profile of v0, /device:TPU:1, one launch (start us, length us, event | category | flops | bytes accessed | tf_op | source)
XLA Modules:
  0.0 483.0 jit_solution(17349624156168429195)
XLA Ops:
  7.2 0.0 copy-start
  7.2 0.0 copy-start.4
  7.2 0.0 all-reduce.5.cloned.1.call-start
  7.2 0.7 convert_log_fusion.1
  8.0 0.7 convert_log_fusion
  8.7 0.0 copy-done
  8.7 1.6 subtract_reduce_fusion.1
  10.3 0.0 copy-start.1
  10.3 0.0 copy-done.4
  10.3 0.0 copy-start.3
  10.3 1.8 select_reduce_fusion.1
  12.2 29.4 %all-gather.7 = f32[16,1,512]{2,1,0:T(1,128)S(1)} all-gather(f32[1,1,512]{2,1,0:T(1,128)S(1)} %bitcast.73), channel_id=3, replica_groups=mesh['row'=32,'col'=16] {'col'}, dimensions={0}, use_global_device_ids=true | all-gather | bytes 34816 | tf_op jit(solution)/shard_map/all_gather | solution.py:8
  41.6 19.1 %all-gather.8 = f32[16,1,512]{2,1,0:T(1,128)S(1)} all-gather(f32[1,1,512]{2,1,0:T(1,128)S(1)} %bitcast.72), channel_id=4, replica_groups=mesh['row'=32,'col'=16] {'col'}, dimensions={0}, use_global_device_ids=true | all-gather | bytes 34816 | tf_op jit(solution)/shard_map/all_gather | solution.py:8
  60.7 21.0 %all-gather.9 = f32[16,1,512]{2,1,0:T(1,128)S(1)} all-gather(f32[1,1,512]{2,1,0:T(1,128)S(1)} %bitcast.71), channel_id=5, replica_groups=mesh['row'=32,'col'=16] {'col'}, dimensions={0}, use_global_device_ids=true | all-gather | bytes 34816 | tf_op jit(solution)/shard_map/all_gather | solution.py:8
  81.7 19.1 %all-gather.6 = f32[16,1,512]{2,1,0:T(1,128)S(1)} all-gather(f32[1,1,512]{2,1,0:T(1,128)S(1)} %bitcast.70), channel_id=2, replica_groups=mesh['row'=32,'col'=16] {'col'}, dimensions={0}, use_global_device_ids=true | all-gather | bytes 34816 | tf_op jit(solution)/shard_map/all_gather | solution.py:8
  100.8 53.4 %all-gather.10 = f32[32,1,1024]{2,1,0:T(1,128)S(1)} all-gather(f32[1,1,1024]{2,1,0:T(1,128)S(1)} %bitcast.69), channel_id=1, replica_groups=mesh['row'=32,'col'=16] {'row'}, dimensions={0}, use_global_device_ids=true | all-gather | bytes 135168 | tf_op jit(solution)/shard_map/all_gather | solution.py:8
  154.2 23.9 %all-gather.4 = f32[32768]{0:T(1024)S(1)} all-gather(f32[1024]{0:T(1024)S(1)} %broadcast_maximum_fusion), channel_id=6, replica_groups=mesh['row'=32,'col'=16] {'row'}, dimensions={0}, use_global_device_ids=true | all-gather | bytes 135168 | tf_op jit(solution)/shard_map/all_gather | solution.py:8
  178.2 22.4 %all-gather.5 = f32[32768]{0:T(1024)S(1)} all-gather(f32[1024]{0:T(1024)S(1)} %get-tuple-element.495), channel_id=7, replica_groups=mesh['row'=32,'col'=16] {'row'}, dimensions={0}, use_global_device_ids=true | all-gather | bytes 135168 | tf_op jit(solution)/shard_map/all_gather | solution.py:8
  200.6 0.0 copy-start.2
  200.6 0.0 copy-done.1
  200.6 1.6 while.12
  202.3 2.9 while.26
  205.2 0.6 multiply_reduce_fusion
  205.8 0.0 copy-done.3
  205.8 0.6 add_reduce_fusion
  206.4 2.7 subtract_convert_fusion
  209.1 0.0 copy-done.2
  209.1 1.4 convolution_multiply_fusion.1
  210.5 0.0 all-reduce.5.cloned.1.call-update
  210.5 0.0 all-reduce.3.cloned.1.call-start
  210.6 1.2 convolution_multiply_fusion.2
  211.8 0.0 all-reduce.3.cloned.1.call-update
  213.1 100.6 %psum.23 = f32[]{:T(128)} all-reduce(f32[]{:T(128)S(6)} %add.167), channel_id=1, replica_groups=mesh['row'=32,'col'=16] {'row','col'}, use_global_device_ids=true, to_apply=%region_15.16 | all-reduce | flops 1 | bytes 8 | tf_op jit(solution)/shard_map/psum | solution.py:88
  314.4 26.3 %all-reduce.5.cloned.1.call-done = f32[1024,256]{1,0:T(8,128)} async-done(((f32[1024,256]{1,0:T(8,128)}), f32[1024,256]{1,0:T(8,128)}) %all-reduce.5.cloned.1.call-update) | async-done | bytes 1048592 | tf_op jit(solution)/shard_map/psum | solution.py:113
  340.7 130.2 %all-reduce.3.cloned.1.call-done = f32[512,256]{1,0:T(8,128)} async-done(((f32[512,256]{1,0:T(8,128)}), f32[512,256]{1,0:T(8,128)}) %all-reduce.3.cloned.1.call-update) | async-done | bytes 524304 | tf_op jit(solution)/shard_map/psum | solution.py:112
  470.9 1.9 copy.52
  472.8 2.3 copy.53
  (216 shorter events, 2.5 us)
Async XLA Ops:
  7.2 1.5 copy-start
  7.2 3.1 copy-start.4
  7.2 333.5 %all-reduce.5.cloned.1.call-start = ((), (), s32[]{:S(2)}) async-start(), calls=%async_computation.1 | async-start | bytes 2097152 | tf_op jit(solution)/shard_map/psum | solution.py:113
  10.3 190.4 %copy-start.1 = (f32[512,1024]{1,0:T(8,128)}, f32[512,1024]{1,0:T(8,128)S(1)}, u32[]{:S(2)}) copy-start(f32[512,1024]{1,0:T(8,128)S(1)} %get-tuple-element.542) | copy-start | bytes 6291460
  10.3 195.5 %copy-start.3 = (s32[512]{0:T(512)S(1)}, s32[512]{0:T(512)}, u32[]{:S(2)}) copy-start(s32[512]{0:T(512)} %param.12) | copy-start | bytes 6148
  200.6 8.4 %copy-start.2 = (bf16[512,256]{1,0:T(8,128)(2,1)S(1)}, bf16[512,256]{1,0:T(8,128)(2,1)}, u32[]{:S(2)}) copy-start(bf16[512,256]{1,0:T(8,128)(2,1)} %param.9) | copy-start | bytes 786436
  210.5 260.4 %all-reduce.3.cloned.1.call-start = ((), (), s32[]{:S(2)}) async-start(), calls=%async_computation | async-start | bytes 1048576 | tf_op jit(solution)/shard_map/psum | solution.py:112
Sparse Core Ops, SparseCore 0:
  210.7 130.0 all-reduce.4
  343.7 127.1 all-reduce.2
where the time goes:
time: 492 us; the launch traced here: 483 us
  blocking collectives  289 us (59%)
  waiting for transfers between devices  157 us (32%)
  between operations  17.2 us (3%)
  other arithmetic  8.3 us (2%)
  local copies, waits for them, and re-layouts  5.54 us (1%)
    all_gather x7, blocking collectives, joined(): everything = jax.tree.map(lambda part: lax.all_gather(part, axis), array)  188 us
    psum x1, waiting for transfers between devices, per_device(): user_grad = lax.psum(user_parts.reshape(rows_here, width), 'col')  130 us
    psum x1, blocking collectives, per_device(): lax.psum(local_loss, ('row', 'col')) / (rows_here * lax.axis_size('row'))  101 us
    psum x1, waiting for transfers between devices, per_device(): item_grad = lax.psum(item_acc, 'row')  26.3 us
  transfers between devices with their start and end apart: 2, of which 2 were waited for; matrix products, arithmetic and copies ran while one was open for 0% of the time, Pallas kernels for 0%

commit v1 on v0

v1 whole, which is shorter than its diff:
```python
import functools

import jax
import jax.numpy as jnp
from jax import lax
from jax.experimental import pallas as pl
from jax.experimental.pallas import tpu as pltpu
from jax.sharding import PartitionSpec as P

MESH = pl.DeviceIdType.MESH
LANES = 128
BLOCK = 128
F32 = jnp.float32


def columns_of(row):
    return jnp.transpose(jnp.broadcast_to(row, (LANES, LANES)))


def fold(block):
    return block.reshape(block.shape[0] // 8, 8, LANES)


def merged_lse(parts):
    top = jnp.max(parts, axis=0)
    return top + jnp.log(jnp.sum(jnp.exp(parts - top[None]), axis=0))


def kernel(
    total_users,
    chips,
    rings,
    user_ref,
    item_ref,
    pos_ref,
    ucnt_ref,
    icnt_ref,
    ug_ref,
    ig_ref,
    loss_ref,
    scores,
    coupling,
    part,
    items,
    log_item,
    lu_col,
    pos_col,
    row_col,
    col_max,
    col_sum,
    hits_acc,
    z_stats,
    c_stats,
    p_stats,
    z_loss,
    plus_in,
    minus_in,
    core_in,
    plane_out,
    plane_in,
    z_sems,
    c_sems,
    p_sems,
    l_sems,
    plus_sems,
    minus_sems,
    gplus_sems,
    gminus_sems,
    x_sems,
):
    rows_here, width = user_ref.shape
    cols_here = item_ref.shape[0]
    tiles = cols_here // LANES
    row_tiles = rows_here // LANES
    half_cols = cols_here // 2
    half_tiles = tiles // 2
    blocks = rows_here // BLOCK
    chunk = rows_here // rings
    piece = half_cols // chips
    half = rings // 2

    mine = lax.axis_index("row")
    ring = lax.axis_index("col")
    chip = mine // 2
    core = mine % 2
    other = 1 - core
    twin = chip * 2 + other

    def z_peer(step):
        return (mine, (ring + step) % rings)

    def chip_peer(step):
        return (((chip + step) % chips) * 2 + core, ring)

    z_steps = sorted(range(1, rings), key=lambda k: -min(k, rings - k))
    chip_steps = list(range(1, chips))

    barrier = pltpu.get_barrier_semaphore()
    for step in z_steps:
        pl.semaphore_signal(barrier, inc=1, device_id=z_peer(step), device_id_type=MESH)
    for step in chip_steps:
        pl.semaphore_signal(barrier, inc=1, device_id=chip_peer(step), device_id_type=MESH)
    pl.semaphore_signal(barrier, inc=1, device_id=(twin, ring), device_id_type=MESH)

    def remote(src, dst, send_sem, recv_sem, device):
        return pltpu.make_async_remote_copy(
            src_ref=src,
            dst_ref=dst,
            send_sem=send_sem,
            recv_sem=recv_sem,
            device_id=device,
            device_id_type=MESH,
        )

    def wait_bytes(ref, sem):
        pltpu.make_async_copy(ref, ref, sem).wait()

    log_item[...] = jnp.log(icnt_ref[...].astype(F32))
    log_user = jnp.log(ucnt_ref[...].astype(F32))
    local_pos = pos_ref[...].astype(F32) - (ring * cols_here).astype(F32)
    for k in range(row_tiles):
        span = pl.ds(k * LANES, LANES)
        lu_col[span, :] = columns_of(log_user[k : k + 1, :])
        pos_col[span, :] = columns_of(local_pos[k : k + 1, :])
    col_max[...] = jnp.full(col_max.shape, -jnp.inf, F32)
    col_sum[...] = jnp.zeros(col_sum.shape, F32)
    hits_acc[...] = jnp.zeros(hits_acc.shape, F32)
    lane = lax.broadcasted_iota(jnp.int32, (BLOCK, LANES), 1).astype(F32)

    def sweep_one(b, z_part):
        span = pl.ds(pl.multiple_of(b * BLOCK, BLOCK), BLOCK)
        scores[span, :] = 2.0 * lax.dot_general(
            user_ref[span, :],
            item_ref[...],
            (((1,), (1,)), ((), ())),
            preferred_element_type=F32,
        )
        lu = lu_col[span, :]
        pos = pos_col[span, :]
        top = None
        for t in range(tiles):
            s = scores[span, t * LANES : (t + 1) * LANES]
            shifted = s - log_item[t : t + 1, :]
            top = shifted if top is None else jnp.maximum(top, shifted)
            col_max[t] = jnp.maximum(col_max[t], jnp.max(fold(s - lu), axis=0))
            match = pos == lane + float(t * LANES)
            hits_acc[t] += jnp.sum(fold(jnp.where(match, 1.0, 0.0)), axis=0)
            z_part = z_part + jnp.sum(fold(jnp.where(match, s + shifted, 0.0)), axis=0)
        row_col[span, :] = jnp.broadcast_to(jnp.max(top, axis=1, keepdims=True), (BLOCK, LANES))
        return z_part

    z_part = lax.fori_loop(0, blocks, sweep_one, jnp.zeros((8, LANES), F32))
    for t in range(tiles):
        col_max[t] = jnp.broadcast_to(jnp.max(col_max[t], axis=0, keepdims=True), (8, LANES))

    z_stats[ring] = jnp.zeros((8, LANES), F32)

    def sweep_two(b, carry):
        span = pl.ds(pl.multiple_of(b * BLOCK, BLOCK), BLOCK)
        lu = lu_col[span, :]
        row_max = row_col[span, :]
        total = jnp.zeros((BLOCK, LANES), F32)
        for t in range(tiles):
            s = scores[span, t * LANES : (t + 1) * LANES]
            total = total + jnp.exp(s - log_item[t : t + 1, :] - row_max)
            col = jnp.exp(fold(s - lu) - col_max[t][None])
            col_sum[t] += jnp.sum(col, axis=0)
        lse = row_max + jnp.log(jnp.sum(total, axis=1, keepdims=True))
        z_stats[ring, pl.ds(b, 1), :] = jnp.transpose(lse)[0:1, :]
        return carry

    lax.fori_loop(0, blocks, sweep_two, 0)
    z_stats[ring, pl.ds(row_tiles, 1), :] = jnp.sum(z_part, axis=0, keepdims=True)
    col_lse_rows = []
    hits_rows = []
    for t in range(tiles):
        total = jnp.sum(col_sum[t], axis=0, keepdims=True)
        col_lse_rows.append(col_max[t, 0:1, :] + jnp.log(total))
        hits_rows.append(jnp.sum(hits_acc[t], axis=0, keepdims=True))
    c_stats[0] = jnp.concatenate(col_lse_rows + hits_rows, axis=0)

    pl.semaphore_wait(barrier, rings - 1 + chips - 1 + 1)
    core_stat = remote(c_stats.at[0], c_stats.at[1], c_sems.at[0], c_sems.at[1], (twin, ring))
    core_stat.start()
    for step in z_steps:
        remote(
            z_stats.at[ring], z_stats.at[ring], z_sems.at[0], z_sems.at[1], z_peer(step)
        ).start()
    core_stat.wait()
    one, two = c_stats[0], c_stats[1]
    p_stats[chip, 0:tiles, :] = merged_lse(jnp.stack([one[:tiles], two[:tiles]]))
    p_stats[chip, tiles : 2 * tiles, :] = one[tiles:] + two[tiles:]
    for step in chip_steps:
        remote(
            p_stats.at[chip], p_stats.at[chip], p_sems.at[0], p_sems.at[1], chip_peer(step)
        ).start()
    wait_bytes(z_stats.at[pl.ds(0, rings - 1)], z_sems.at[1])
    user_stats = z_stats[...]
    row_lse = merged_lse(user_stats[:, :row_tiles])
    for k in range(row_tiles):
        row_col[pl.ds(k * LANES, LANES), :] = columns_of(row_lse[k : k + 1, :])
    user_loss = jnp.sum(row_lse + log_user, axis=0, keepdims=True) - jnp.sum(
        user_stats[:, row_tiles : row_tiles + 1], axis=0
    )
    wait_bytes(p_stats.at[pl.ds(0, chips - 1)], p_sems.at[1])
    item_stats = p_stats[...]
    col_lse = merged_lse(item_stats[:, :tiles])
    pos_hits = jnp.sum(item_stats[:, tiles:], axis=0)
    z_loss[ring] = jnp.broadcast_to(
        jnp.sum(pos_hits * col_lse, axis=0, keepdims=True), (8, LANES)
    )

    def sweep_three(b, carry):
        span = pl.ds(pl.multiple_of(b * BLOCK, BLOCK), BLOCK)
        lu = lu_col[span, :]
        pos = pos_col[span, :]
        row = row_col[span, :]
        for t in range(tiles):
            s = scores[span, t * LANES : (t + 1) * LANES]
            value = jnp.exp(s - log_item[t : t + 1, :] - row) + pos_hits[t : t + 1, :] * jnp.exp(
                s - lu - col_lse[t : t + 1, :]
            )
            match = pos == lane + float(t * LANES)
            value = value - jnp.where(match, 2.0, 0.0)
            place = (t % half_tiles) * LANES
            coupling[t // half_tiles, span, place : place + LANES] = value.astype(jnp.bfloat16)
        part[span, :] = 2.0 * (
            jnp.dot(coupling[0, span, :], item_ref[:half_cols, :], preferred_element_type=F32)
            + jnp.dot(coupling[1, span, :], item_ref[half_cols:, :], preferred_element_type=F32)
        )
        return carry

    lax.fori_loop(0, blocks, sweep_three, 0)

    def chunk_at(index):
        return pl.ds(pl.multiple_of(index % rings * chunk, chunk), chunk)

    up = z_peer(1)
    down = z_peer(rings - 1)

    def reduce_step(step):
        if step < half:
            span = chunk_at(ring + half - step)
            if step == 0:
                src = part.at[span, :]
            else:
                src = plus_in.at[step - 1]
                wait_bytes(src, plus_sems.at[1, step - 1])
                plus_in[step - 1] += part[span, :]
            remote(
                src, plus_in.at[step], plus_sems.at[0, step], plus_sems.at[1, step], up
            ).start()
        if step < half - 1:
            span = chunk_at(ring + rings - (half - 1) + step)
            if step == 0:
                src = part.at[span, :]
            else:
                src = minus_in.at[step - 1]
                wait_bytes(src, minus_sems.at[1, step - 1])
                minus_in[step - 1] += part[span, :]
            remote(
                src, minus_in.at[step], minus_sems.at[0, step], minus_sems.at[1, step], down
            ).start()

    def reduce_end():
        wait_bytes(minus_in.at[half - 2], minus_sems.at[1, half - 2])
        wait_bytes(plus_in.at[half - 1], plus_sems.at[1, half - 1])
        span = chunk_at(ring)
        ug_ref[span, :] = part[span, :] + plus_in[half - 1] + minus_in[half - 2]

    def gather_step(step):
        if step < half:
            if step > 0:
                span = chunk_at(ring + rings - step)
                wait_bytes(ug_ref.at[span, :], gplus_sems.at[1, step - 1])
            span = chunk_at(ring + rings - step)
            here = ug_ref.at[span, :]
            remote(here, here, gplus_sems.at[0, step], gplus_sems.at[1, step], up).start()
        if step < half - 1:
            span = chunk_at(ring + step)
            here = ug_ref.at[span, :]
            if step > 0:
                wait_bytes(here, gminus_sems.at[1, step - 1])
            remote(here, here, gminus_sems.at[0, step], gminus_sems.at[1, step], down).start()

    def gather_end():
        wait_bytes(ug_ref.at[chunk_at(ring + half), :], gplus_sems.at[1, half - 1])
        wait_bytes(ug_ref.at[chunk_at(ring + half - 1), :], gminus_sems.at[1, half - 2])

    def item_part(which):
        items[which, :half_cols, :] = 2.0 * lax.dot_general(
            coupling[which],
            user_ref[...],
            (((0,), (0,)), ((), ())),
            preferred_element_type=F32,
        )

    core_copy = remote(items.at[other], core_in, x_sems.at[0], x_sems.at[1], (twin, ring))

    def core_send():
        item_part(other)
        items[other, half_cols:, :LANES] = jnp.broadcast_to(user_loss, (8, LANES))
        items[other, half_cols:, LANES:] = jnp.zeros((8, width - LANES), F32)
        core_copy.start()

    def loss_send():
        for step in z_steps:
            remote(
                z_loss.at[ring], z_loss.at[ring], l_sems.at[0], l_sems.at[1], z_peer(step)
            ).start()

    def plane_send():
        core_copy.wait_recv()
        pair_loss = core_in[half_cols:, :LANES] + user_loss

        def pack(k, carry):
            span = pl.ds(pl.multiple_of(k * piece, piece), piece)
            plane_out[k, :piece, :] = items[core, span, :] + core_in[span, :]
            plane_out[k, piece:, :LANES] = pair_loss
            plane_out[k, piece:, LANES:] = jnp.zeros((8, width - LANES), F32)
            return carry

        lax.fori_loop(0, chips, pack, 0)
        for step in chip_steps:
            remote(
                plane_out.at[(chip + step) % chips],
                plane_in.at[chip],
                x_sems.at[2],
                x_sems.at[3],
                chip_peer(step),
            ).start()
        plane_in[chip] = plane_out[chip]

    def piece_at(half_index, index):
        return pl.ds(pl.multiple_of(half_index * half_cols + index * piece, piece), piece)

    def plane_sum():
        wait_bytes(plane_in.at[pl.ds(0, chips - 1)], x_sems.at[3])
        total = plane_in[0]
        for k in range(1, chips):
            total = total + plane_in[k]
        here = ig_ref.at[piece_at(core, chip), :]
        here[...] = total[:piece, :]
        for step in chip_steps:
            remote(here, here, x_sems.at[4], x_sems.at[5], chip_peer(step)).start()
        return total[piece : piece + 1, :LANES]

    half_here = ig_ref.at[pl.ds(pl.multiple_of(core * half_cols, half_cols), half_cols), :]
    half_copy = remote(half_here, half_here, x_sems.at[6], x_sems.at[7], (twin, ring))
    others = pl.ds(0, (chips - 1) * piece)

    def half_send():
        wait_bytes(ig_ref.at[others, :], x_sems.at[5])
        half_copy.start()

    def loss_end(users):
        wait_bytes(z_loss.at[pl.ds(0, rings - 1)], l_sems.at[1])
        total = users
        for k in range(rings):
            total = total + z_loss[k, 0:1, :]
        loss_ref[0, 0] = jnp.sum(total) * (1.0 / total_users)

    events = []
    for step in range(half):
        events.append(functools.partial(reduce_step, step))
    events.append(reduce_end)
    for step in range(half):
        events.append(functools.partial(gather_step, step))
    events.append(gather_end)
    state = {}

    def sum_event():
        state["users"] = plane_sum()

    def loss_event():
        loss_end(state["users"])

    last = len(events) - 1
    extra = {}
    for place, event in (
        (0, core_send),
        (1, lambda: item_part(core)),
        (1, loss_send),
        (2, plane_send),
        (half + 1, sum_event),
        (half + 2, loss_event),
        (half + 5, half_send),
    ):
        extra.setdefault(min(place, last - 1), []).append(event)
    for place, event in enumerate(events):
        event()
        for more in extra.get(place, ()):
            more()
    half_copy.wait_recv()

    wait_bytes(z_stats.at[pl.ds(0, rings - 1)], z_sems.at[0])
    wait_bytes(p_stats.at[pl.ds(0, chips - 1)], p_sems.at[0])
    wait_bytes(z_loss.at[pl.ds(0, rings - 1)], l_sems.at[0])
    for step in range(half):
        wait_bytes(plus_in.at[step], plus_sems.at[0, step])
        wait_bytes(plus_in.at[step], gplus_sems.at[0, step])
    for step in range(half - 1):
        wait_bytes(minus_in.at[step], minus_sems.at[0, step])
        wait_bytes(minus_in.at[step], gminus_sems.at[0, step])
    core_copy.wait_send()
    wait_bytes(plane_in.at[pl.ds(0, chips - 1)], x_sems.at[2])
    wait_bytes(ig_ref.at[others, :], x_sems.at[4])
    half_copy.wait_send()


def per_device(total_users, chips, rings, user_embed, item_embed, positive, user_count, item_count):
    rows, width = user_embed.shape
    cols = item_embed.shape[0]
    tiles = cols // LANES
    half = rings // 2
    chunk = rows // rings
    piece = cols // 2 // chips
    vmem = pl.BlockSpec(memory_space=pltpu.VMEM)
    dma = pltpu.SemaphoreType.DMA
    user_grad, item_grad, loss = pl.pallas_call(
        functools.partial(kernel, total_users, chips, rings),
        out_shape=(
            jax.ShapeDtypeStruct((rows, width), F32),
            jax.ShapeDtypeStruct((cols, width), F32),
            jax.ShapeDtypeStruct((1, 1), F32),
        ),
        in_specs=[vmem] * 5,
        out_specs=(vmem, vmem, pl.BlockSpec(memory_space=pltpu.SMEM)),
        scratch_shapes=[
            pltpu.VMEM((rows, cols), F32),
            pltpu.VMEM((2, rows, cols // 2), jnp.bfloat16),
            pltpu.VMEM((rows, width), F32),
            pltpu.VMEM((2, cols // 2 + 8, width), F32),
            pltpu.VMEM((tiles, LANES), F32),
            pltpu.VMEM((rows, LANES), F32),
            pltpu.VMEM((rows, LANES), F32),
            pltpu.VMEM((rows, LANES), F32),
            pltpu.VMEM((tiles, 8, LANES), F32),
            pltpu.VMEM((tiles, 8, LANES), F32),
            pltpu.VMEM((tiles, 8, LANES), F32),
            pltpu.VMEM((rings, 8, LANES), F32),
            pltpu.VMEM((2, 2 * tiles, LANES), F32),
            pltpu.VMEM((chips, 2 * tiles, LANES), F32),
            pltpu.VMEM((rings, 8, LANES), F32),
            pltpu.VMEM((half, chunk, width), F32),
            pltpu.VMEM((half - 1, chunk, width), F32),
            pltpu.VMEM((cols // 2 + 8, width), F32),
            pltpu.VMEM((chips, piece + 8, width), F32),
            pltpu.VMEM((chips, piece + 8, width), F32),
            dma((2,)),
            dma((2,)),
            dma((2,)),
            dma((2,)),
            dma((2, half)),
            dma((2, half - 1)),
            dma((2, half)),
            dma((2, half - 1)),
            dma((8,)),
        ],
        compiler_params=pltpu.CompilerParams(
            collective_id=0, has_side_effects=True, vmem_limit_bytes=40 * 1024 * 1024
        ),
        name="two_sided",
    )(
        user_embed,
        item_embed,
        positive.reshape(rows // LANES, LANES),
        user_count.reshape(rows // LANES, LANES),
        item_count.reshape(tiles, LANES),
    )
    return user_grad, item_grad, loss.reshape(())


def solution(mesh):
    row_size, rings = mesh.shape["row"], mesh.shape["col"]

    def whole(user_embed, *others):
        body = functools.partial(per_device, user_embed.shape[0], row_size // 2, rings)
        return jax.shard_map(
            body,
            mesh=mesh,
            in_specs=(P("row", None), P("col", None), P("row"), P("row"), P("col")),
            out_specs=(P("row", None), P("col", None), P()),
            check_vma=False,
        )(user_embed, *others)

    return whole
```

time: 492 us -> 83.5 us (0.17)
  the two profiles are of different devices: /device:TPU:1 before, /device:TPU:32 now
where the time goes in v1:
time: 83.5 us; the launch traced here: 83.2 us
  Pallas kernels  75.1 us (90%)
  local copies, waits for them, and re-layouts  5.8 us (7%)
  between operations  2.34 us (3%)
    pallas_call x1, Pallas kernels, per_device(): pl.pallas_call(functools.partial(kernel, total_users, chips, rings), out_...  75.1 us
    unnamed x12, local copies, waits for them, and re-layouts  5.8 us

profile of v1, /device:TPU:32, one launch (start us, length us, event | category | flops | bytes accessed | tf_op | source)
XLA Modules:
  0.0 83.2 jit_solution(12633393370207304200)
XLA Ops:
  0.6 0.0 copy-start.2
  0.6 0.7 copy-done.2
  1.3 0.0 copy-start
  1.3 1.0 %copy-done = bf16[1024,256]{1,0:T(8,128)(2,1)S(1)} copy-done((bf16[1024,256]{1,0:T(8,128)(2,1)S(1)}, bf16[1024,256]{1,0:T(8,128)(2,1)}, u32[]{:S(2)}) %copy-start) | copy-done | bytes 524312
  2.4 0.0 copy-start.1
  2.4 0.9 %copy-done.1 = bf16[512,256]{1,0:T(8,128)(2,1)S(1)} copy-done((bf16[512,256]{1,0:T(8,128)(2,1)S(1)}, bf16[512,256]{1,0:T(8,128)(2,1)}, u32[]{:S(2)}) %copy-start.1) | copy-done | bytes 262168
  3.3 0.0 copy-start.3
  3.3 0.7 copy-done.3
  4.0 0.0 copy-start.4
  4.0 0.7 copy-done.4
  4.7 75.1 %two_sided.1 = (f32[512,256]{1,0:T(8,128)S(1)}, f32[1024,256]{1,0:T(8,128)S(1)}, f32[1,1]{1,0:T(1,128)}) custom-call(bf16[512,256]{1,0:T(8,128)(2,1)S(1)} %copy-done.1, bf16[1024,256]{1,0:T(8,128)(2,1)S(1)} %copy-done, s32[4,128]{1,0:T(4,128)S(1)} %bitcast.5, s32[4,128]{1,0:T(4,128)S(1)} %bitcast.6, s32[8,128]{1,0:T(8,128)S(1)} %bitcast.4), custom_call_target="tpu_custom_call" | custom-call | tf_op jit(solution)/shard_map/two_sided/pallas_call | solution.py:420
  79.7 0.8 copy.11
  80.5 1.0 %copy.12 = f32[1024,256]{1,0:T(8,128)} copy(f32[1024,256]{1,0:T(8,128)S(1)} %get-tuple-element.13) | data formatting | bytes 2097152
Async XLA Ops:
  0.6 0.7 copy-start.2
  1.3 1.0 %copy-start = (bf16[1024,256]{1,0:T(8,128)(2,1)S(1)}, bf16[1024,256]{1,0:T(8,128)(2,1)}, u32[]{:S(2)}) copy-start(bf16[1024,256]{1,0:T(8,128)(2,1)} %item_ref.1) | copy-start | bytes 1572868
  2.4 0.9 %copy-start.1 = (bf16[512,256]{1,0:T(8,128)(2,1)S(1)}, bf16[512,256]{1,0:T(8,128)(2,1)}, u32[]{:S(2)}) copy-start(bf16[512,256]{1,0:T(8,128)(2,1)} %user_ref.1) | copy-start | bytes 786436
  3.3 0.7 copy-start.3
  4.0 0.7 copy-start.4

commit v2 on v1

--- a/solution.py
+++ b/solution.py
@@ -10,6 +10,8 @@
 MESH = pl.DeviceIdType.MESH
 LANES = 128
 BLOCK = 128
+WINDOW = 4
+CORE_PARTS = 4
 F32 = jnp.float32
 
 
@@ -30,14 +32,16 @@
     total_users,
     chips,
     rings,
-    user_ref,
-    item_ref,
+    user_hbm,
+    item_hbm,
     pos_ref,
     ucnt_ref,
     icnt_ref,
     ug_ref,
     ig_ref,
     loss_ref,
+    user_ref,
+    item_ref,
     scores,
     coupling,
     part,
@@ -53,8 +57,8 @@
     c_stats,
     p_stats,
     z_loss,
-    plus_in,
-    minus_in,
+    window_in,
+    stride_in,
     core_in,
     plane_out,
     plane_in,
@@ -62,11 +66,11 @@
     c_sems,
     p_sems,
     l_sems,
-    plus_sems,
-    minus_sems,
-    gplus_sems,
-    gminus_sems,
+    w_sems,
+    g_sems,
     x_sems,
+    back_sems,
+    in_sems,
 ):
     rows_here, width = user_ref.shape
     cols_here = item_ref.shape[0]
@@ -75,9 +79,12 @@
     half_cols = cols_here // 2
     half_tiles = tiles // 2
     blocks = rows_here // BLOCK
-    chunk = rows_here // rings
     piece = half_cols // chips
-    half = rings // 2
+
+    user_in = pltpu.make_async_copy(user_hbm, user_ref, in_sems.at[0])
+    item_in = pltpu.make_async_copy(item_hbm, item_ref, in_sems.at[1])
+    item_in.start()
+    user_in.start()
 
     mine = lax.axis_index("row")
     ring = lax.axis_index("col")
@@ -149,6 +156,8 @@
         row_col[span, :] = jnp.broadcast_to(jnp.max(top, axis=1, keepdims=True), (BLOCK, LANES))
         return z_part
 
+    item_in.wait()
+    user_in.wait()
     z_part = lax.fori_loop(0, blocks, sweep_one, jnp.zeros((8, LANES), F32))
     for t in range(tiles):
         col_max[t] = jnp.broadcast_to(jnp.max(col_max[t], axis=0, keepdims=True), (8, LANES))
@@ -210,8 +219,24 @@
         jnp.sum(pos_hits * col_lse, axis=0, keepdims=True), (8, LANES)
     )
 
-    def sweep_three(b, carry):
-        span = pl.ds(pl.multiple_of(b * BLOCK, BLOCK), BLOCK)
+    group = rings // WINDOW
+    strip = BLOCK // group
+    place = ring // WINDOW
+    halves = (pl.ds(0, BLOCK // 2), pl.ds(BLOCK // 2, BLOCK // 2))
+
+    def block_at(index):
+        return pl.ds(pl.multiple_of(index % WINDOW * BLOCK, BLOCK), BLOCK)
+
+    def half_at(index, k):
+        start = index % WINDOW * BLOCK + k * (BLOCK // 2)
+        return pl.ds(pl.multiple_of(start, BLOCK // 2), BLOCK // 2)
+
+    def strip_at(index, k):
+        start = index % WINDOW * BLOCK + k % group * strip
+        return pl.ds(pl.multiple_of(start, strip), strip)
+
+    def user_block(index):
+        span = block_at(index)
         lu = lu_col[span, :]
         pos = pos_col[span, :]
         row = row_col[span, :]
@@ -222,70 +247,79 @@
             )
             match = pos == lane + float(t * LANES)
             value = value - jnp.where(match, 2.0, 0.0)
-            place = (t % half_tiles) * LANES
-            coupling[t // half_tiles, span, place : place + LANES] = value.astype(jnp.bfloat16)
+            at = (t % half_tiles) * LANES
+            coupling[t // half_tiles, span, at : at + LANES] = value.astype(jnp.bfloat16)
         part[span, :] = 2.0 * (
             jnp.dot(coupling[0, span, :], item_ref[:half_cols, :], preferred_element_type=F32)
             + jnp.dot(coupling[1, span, :], item_ref[half_cols:, :], preferred_element_type=F32)
         )
-        return carry
-
-    lax.fori_loop(0, blocks, sweep_three, 0)
-
-    def chunk_at(index):
-        return pl.ds(pl.multiple_of(index % rings * chunk, chunk), chunk)
-
-    up = z_peer(1)
-    down = z_peer(rings - 1)
-
-    def reduce_step(step):
-        if step < half:
-            span = chunk_at(ring + half - step)
-            if step == 0:
-                src = part.at[span, :]
-            else:
-                src = plus_in.at[step - 1]
-                wait_bytes(src, plus_sems.at[1, step - 1])
-                plus_in[step - 1] += part[span, :]
+
+    near = ((1, 0), (rings - 1, 1))
+
+    def window_send(step, slot):
+        for k in range(2):
             remote(
-                src, plus_in.at[step], plus_sems.at[0, step], plus_sems.at[1, step], up
+                part.at[half_at(ring + step, k), :],
+                window_in.at[slot, halves[k], :],
+                w_sems.at[0],
+                w_sems.at[1],
+                z_peer(step),
             ).start()
-        if step < half - 1:
-            span = chunk_at(ring + rings - (half - 1) + step)
-            if step == 0:
-                src = part.at[span, :]
-            else:
-                src = minus_in.at[step - 1]
-                wait_bytes(src, minus_sems.at[1, step - 1])
-                minus_in[step - 1] += part[span, :]
+
+    for step, slot in near:
+        user_block(ring + step)
+        window_send(step, slot)
+    user_block(ring + 2)
+    for k, step in enumerate((2, rings - 2)):
+        remote(
+            part.at[half_at(ring + 2, k), :],
+            window_in.at[2, halves[k], :],
+            w_sems.at[0],
+            w_sems.at[1],
+            z_peer(step),
+        ).start()
+    user_block(ring)
+
+    def stride_send():
+        wait_bytes(window_in, w_sems.at[1])
+        span = block_at(ring)
+        part[span, :] += window_in[0] + window_in[1] + window_in[2]
+        for k in range(1, group):
             remote(
-                src, minus_in.at[step], minus_sems.at[0, step], minus_sems.at[1, step], down
+                part.at[strip_at(ring, place + k), :],
+                stride_in.at[k - 1],
+                w_sems.at[2],
+                w_sems.at[3],
+                z_peer(k * WINDOW),
             ).start()
 
-    def reduce_end():
-        wait_bytes(minus_in.at[half - 2], minus_sems.at[1, half - 2])
-        wait_bytes(plus_in.at[half - 1], plus_sems.at[1, half - 1])
-        span = chunk_at(ring)
-        ug_ref[span, :] = part[span, :] + plus_in[half - 1] + minus_in[half - 2]
-
-    def gather_step(step):
-        if step < half:
-            if step > 0:
-                span = chunk_at(ring + rings - step)
-                wait_bytes(ug_ref.at[span, :], gplus_sems.at[1, step - 1])
-            span = chunk_at(ring + rings - step)
-            here = ug_ref.at[span, :]
-            remote(here, here, gplus_sems.at[0, step], gplus_sems.at[1, step], up).start()
-        if step < half - 1:
-            span = chunk_at(ring + step)
-            here = ug_ref.at[span, :]
-            if step > 0:
-                wait_bytes(here, gminus_sems.at[1, step - 1])
-            remote(here, here, gminus_sems.at[0, step], gminus_sems.at[1, step], down).start()
+    def spread(index):
+        here = ug_ref.at[strip_at(ring, index), :]
+        for step in (1, rings - 1):
+            remote(here, here, w_sems.at[4], w_sems.at[5], z_peer(step)).start()
+        low = index % group < group // 2
+        far = jnp.where(low, 2, rings - 2)
+        remote(here, here, w_sems.at[4], w_sems.at[5], z_peer(far)).start()
+
+    def stride_sum():
+        wait_bytes(stride_in, w_sems.at[3])
+        span = strip_at(ring, place)
+        total = part[span, :]
+        for k in range(group - 1):
+            total = total + stride_in[k]
+        ug_ref[span, :] = total
+        here = ug_ref.at[span, :]
+        for k in range(1, group):
+            remote(here, here, w_sems.at[6], g_sems.at[k - 1], z_peer(k * WINDOW)).start()
+        spread(place)
+
+    def spread_on(k):
+        index = place + group - k
+        wait_bytes(ug_ref.at[strip_at(ring, index), :], g_sems.at[k - 1])
+        spread(index)
 
     def gather_end():
-        wait_bytes(ug_ref.at[chunk_at(ring + half), :], gplus_sems.at[1, half - 1])
-        wait_bytes(ug_ref.at[chunk_at(ring + half - 1), :], gminus_sems.at[1, half - 2])
+        wait_bytes(ug_ref.at[pl.ds(0, (WINDOW - 1) * BLOCK), :], w_sems.at[5])
 
     def item_part(which):
         items[which, :half_cols, :] = 2.0 * lax.dot_general(
@@ -295,13 +329,22 @@
             preferred_element_type=F32,
         )
 
-    core_copy = remote(items.at[other], core_in, x_sems.at[0], x_sems.at[1], (twin, ring))
+    core_rows = half_cols // CORE_PARTS
 
     def core_send():
         item_part(other)
         items[other, half_cols:, :LANES] = jnp.broadcast_to(user_loss, (8, LANES))
         items[other, half_cols:, LANES:] = jnp.zeros((8, width - LANES), F32)
-        core_copy.start()
+        for k in range(CORE_PARTS):
+            extra = 8 if k == CORE_PARTS - 1 else 0
+            span = pl.ds(k * core_rows, core_rows + extra)
+            remote(
+                items.at[other, span, :],
+                core_in.at[span, :],
+                x_sems.at[0],
+                x_sems.at[1],
+                (twin, ring),
+            ).start()
 
     def loss_send():
         for step in z_steps:
@@ -310,7 +353,7 @@
             ).start()
 
     def plane_send():
-        core_copy.wait_recv()
+        wait_bytes(core_in, x_sems.at[1])
         pair_loss = core_in[half_cols:, :LANES] + user_loss
 
         def pack(k, carry):
@@ -332,7 +375,8 @@
         plane_in[chip] = plane_out[chip]
 
     def piece_at(half_index, index):
-        return pl.ds(pl.multiple_of(half_index * half_cols + index * piece, piece), piece)
+        start = half_index * half_cols + index % chips * piece
+        return pl.ds(pl.multiple_of(start, piece), piece)
 
     def plane_sum():
         wait_bytes(plane_in.at[pl.ds(0, chips - 1)], x_sems.at[3])
@@ -342,16 +386,18 @@
         here = ig_ref.at[piece_at(core, chip), :]
         here[...] = total[:piece, :]
         for step in chip_steps:
-            remote(here, here, x_sems.at[4], x_sems.at[5], chip_peer(step)).start()
+            remote(
+                here, here, x_sems.at[4], back_sems.at[step - 1], chip_peer(step)
+            ).start()
+        remote(here, here, x_sems.at[5], x_sems.at[6], (twin, ring)).start()
         return total[piece : piece + 1, :LANES]
 
-    half_here = ig_ref.at[pl.ds(pl.multiple_of(core * half_cols, half_cols), half_cols), :]
-    half_copy = remote(half_here, half_here, x_sems.at[6], x_sems.at[7], (twin, ring))
+    def forward(step):
+        here = ig_ref.at[piece_at(core, chip + chips - step), :]
+        wait_bytes(here, back_sems.at[step - 1])
+        remote(here, here, x_sems.at[5], x_sems.at[6], (twin, ring)).start()
+
     others = pl.ds(0, (chips - 1) * piece)
-
-    def half_send():
-        wait_bytes(ig_ref.at[others, :], x_sems.at[5])
-        half_copy.start()
 
     def loss_end(users):
         wait_bytes(z_loss.at[pl.ds(0, rings - 1)], l_sems.at[1])
@@ -360,60 +406,38 @@
             total = total + z_loss[k, 0:1, :]
         loss_ref[0, 0] = jnp.sum(total) * (1.0 / total_users)
 
-    events = []
-    for step in range(half):
-        events.append(functools.partial(reduce_step, step))
-    events.append(reduce_end)
-    for step in range(half):
-        events.append(functools.partial(gather_step, step))
-    events.append(gather_end)
-    state = {}
-
-    def sum_event():
-        state["users"] = plane_sum()
-
-    def loss_event():
-        loss_end(state["users"])
-
-    last = len(events) - 1
-    extra = {}
-    for place, event in (
-        (0, core_send),
-        (1, lambda: item_part(core)),
-        (1, loss_send),
-        (2, plane_send),
-        (half + 1, sum_event),
-        (half + 2, loss_event),
-        (half + 5, half_send),
-    ):
-        extra.setdefault(min(place, last - 1), []).append(event)
-    for place, event in enumerate(events):
-        event()
-        for more in extra.get(place, ()):
-            more()
-    half_copy.wait_recv()
+    core_send()
+    item_part(core)
+    loss_send()
+    plane_send()
+    stride_send()
+    stride_sum()
+    loss_end(plane_sum())
+    for k in sorted(range(1, group), key=lambda k: min(k, group - k)):
+        spread_on(k)
+    for step in chip_steps:
+        forward(step)
+    gather_end()
+    wait_bytes(ig_ref.at[pl.ds(0, half_cols), :], x_sems.at[6])
 
     wait_bytes(z_stats.at[pl.ds(0, rings - 1)], z_sems.at[0])
     wait_bytes(p_stats.at[pl.ds(0, chips - 1)], p_sems.at[0])
     wait_bytes(z_loss.at[pl.ds(0, rings - 1)], l_sems.at[0])
-    for step in range(half):
-        wait_bytes(plus_in.at[step], plus_sems.at[0, step])
-        wait_bytes(plus_in.at[step], gplus_sems.at[0, step])
-    for step in range(half - 1):
-        wait_bytes(minus_in.at[step], minus_sems.at[0, step])
-        wait_bytes(minus_in.at[step], gminus_sems.at[0, step])
-    core_copy.wait_send()
+    wait_bytes(window_in, w_sems.at[0])
+    wait_bytes(stride_in, w_sems.at[2])
+    wait_bytes(ug_ref.at[pl.ds(0, (WINDOW - 1) * BLOCK), :], w_sems.at[4])
+    wait_bytes(stride_in, w_sems.at[6])
+    wait_bytes(core_in, x_sems.at[0])
     wait_bytes(plane_in.at[pl.ds(0, chips - 1)], x_sems.at[2])
     wait_bytes(ig_ref.at[others, :], x_sems.at[4])
-    half_copy.wait_send()
+    wait_bytes(ig_ref.at[pl.ds(0, half_cols), :], x_sems.at[5])
 
 
 def per_device(total_users, chips, rings, user_embed, item_embed, positive, user_count, item_count):
     rows, width = user_embed.shape
     cols = item_embed.shape[0]
     tiles = cols // LANES
-    half = rings // 2
-    chunk = rows // rings
+    group = rings // WINDOW
     piece = cols // 2 // chips
     vmem = pl.BlockSpec(memory_space=pltpu.VMEM)
     dma = pltpu.SemaphoreType.DMA
@@ -424,9 +448,11 @@
             jax.ShapeDtypeStruct((cols, width), F32),
             jax.ShapeDtypeStruct((1, 1), F32),
         ),
-        in_specs=[vmem] * 5,
+        in_specs=[pl.BlockSpec(memory_space=pltpu.HBM)] * 2 + [vmem] * 3,
         out_specs=(vmem, vmem, pl.BlockSpec(memory_space=pltpu.SMEM)),
         scratch_shapes=[
+            pltpu.VMEM((rows, width), user_embed.dtype),
+            pltpu.VMEM((cols, width), item_embed.dtype),
             pltpu.VMEM((rows, cols), F32),
             pltpu.VMEM((2, rows, cols // 2), jnp.bfloat16),
             pltpu.VMEM((rows, width), F32),
@@ -442,8 +468,8 @@
             pltpu.VMEM((2, 2 * tiles, LANES), F32),
             pltpu.VMEM((chips, 2 * tiles, LANES), F32),
             pltpu.VMEM((rings, 8, LANES), F32),
-            pltpu.VMEM((half, chunk, width), F32),
-            pltpu.VMEM((half - 1, chunk, width), F32),
+            pltpu.VMEM((WINDOW - 1, BLOCK, width), F32),
+            pltpu.VMEM((group - 1, BLOCK // group, width), F32),
             pltpu.VMEM((cols // 2 + 8, width), F32),
             pltpu.VMEM((chips, piece + 8, width), F32),
             pltpu.VMEM((chips, piece + 8, width), F32),
@@ -451,14 +477,14 @@
             dma((2,)),
             dma((2,)),
             dma((2,)),
-            dma((2, half)),
-            dma((2, half - 1)),
-            dma((2, half)),
-            dma((2, half - 1)),
+            dma((7,)),
+            dma((group - 1,)),
             dma((8,)),
+            dma((chips - 1,)),
+            dma((2,)),
         ],
         compiler_params=pltpu.CompilerParams(
-            collective_id=0, has_side_effects=True, vmem_limit_bytes=40 * 1024 * 1024
+            collective_id=0, has_side_effects=True, vmem_limit_bytes=60 * 1024 * 1024
         ),
         name="two_sided",
     )(

time: 83.5 us -> 64.1 us (0.77)
  the two profiles are of different devices: /device:TPU:32 before, /device:TPU:70 now
where the time goes in v2:
time: 64.1 us; the launch traced here: 63.9 us
  Pallas kernels  58.6 us (91%)
  local copies, waits for them, and re-layouts  2.93 us (5%)
  between operations  2.41 us (4%)
    pallas_call x1, Pallas kernels, per_device(): pl.pallas_call(functools.partial(kernel, total_users, chips, rings), out_...  58.6 us
    unnamed x4, local copies, waits for them, and re-layouts  2.93 us

profile of v2, /device:TPU:70, one launch (start us, length us, event | category | flops | bytes accessed | tf_op | source)
XLA Modules:
  0.0 63.9 jit_solution(12919458984849727007)
XLA Ops:
  0.6 58.6 %two_sided.1 = (f32[512,256]{1,0:T(8,128)}, f32[1024,256]{1,0:T(8,128)}, f32[1,1]{1,0:T(1,128)}) custom-call(bf16[512,256]{1,0:T(8,128)(2,1)} %user_hbm.1, bf16[1024,256]{1,0:T(8,128)(2,1)} %item_hbm.1, s32[4,128]{1,0:T(4,128)} %bitcast.5, s32[4,128]{1,0:T(4,128)} %bitcast.6, s32[8,128]{1,0:T(8,128)} %bitcast.4), custom_call_target="tpu_custom_call" | custom-call | tf_op jit(solution)/shard_map/two_sided/pallas_call | solution.py:444
  59.2 0.0 copy-start
  59.2 2.0 %copy.11 = f32[512,256]{1,0:T(8,128)} copy(f32[512,256]{1,0:T(8,128)} %get-tuple-element.12) | data formatting | bytes 1048576
  61.2 0.0 copy-done
  61.2 1.0 %copy.12 = f32[1024,256]{1,0:T(8,128)} copy(f32[1024,256]{1,0:T(8,128)S(1)} %copy-done) | data formatting | bytes 2097152
Async XLA Ops:
  59.2 2.0 %copy-start = (f32[1024,256]{1,0:T(8,128)S(1)}, f32[1024,256]{1,0:T(8,128)}, u32[]{:S(2)}) copy-start(f32[1024,256]{1,0:T(8,128)} %get-tuple-element.13) | copy-start | bytes 3145732

commit v3 on v2

--- a/solution.py
+++ b/solution.py
@@ -10,7 +10,6 @@
 MESH = pl.DeviceIdType.MESH
 LANES = 128
 BLOCK = 128
-WINDOW = 4
 CORE_PARTS = 4
 F32 = jnp.float32
 
@@ -42,6 +41,7 @@
     loss_ref,
     user_ref,
     item_ref,
+    users,
     scores,
     coupling,
     part,
@@ -54,16 +54,14 @@
     col_sum,
     hits_acc,
     z_stats,
-    c_stats,
     p_stats,
     z_loss,
-    window_in,
-    stride_in,
+    hub_in,
+    near_in,
     core_in,
     plane_out,
     plane_in,
     z_sems,
-    c_sems,
     p_sems,
     l_sems,
     w_sems,
@@ -99,15 +97,18 @@
     def chip_peer(step):
         return (((chip + step) % chips) * 2 + core, ring)
 
+    def row_peer(step):
+        return ((mine + step) % (2 * chips), ring)
+
     z_steps = sorted(range(1, rings), key=lambda k: -min(k, rings - k))
     chip_steps = list(range(1, chips))
+    row_steps = list(range(1, 2 * chips))
 
     barrier = pltpu.get_barrier_semaphore()
     for step in z_steps:
         pl.semaphore_signal(barrier, inc=1, device_id=z_peer(step), device_id_type=MESH)
-    for step in chip_steps:
-        pl.semaphore_signal(barrier, inc=1, device_id=chip_peer(step), device_id_type=MESH)
-    pl.semaphore_signal(barrier, inc=1, device_id=(twin, ring), device_id_type=MESH)
+    for step in row_steps:
+        pl.semaphore_signal(barrier, inc=1, device_id=row_peer(step), device_id_type=MESH)
 
     def remote(src, dst, send_sem, recv_sem, device):
         return pltpu.make_async_remote_copy(
@@ -162,8 +163,6 @@
     for t in range(tiles):
         col_max[t] = jnp.broadcast_to(jnp.max(col_max[t], axis=0, keepdims=True), (8, LANES))
 
-    z_stats[ring] = jnp.zeros((8, LANES), F32)
-
     def sweep_two(b, carry):
         span = pl.ds(pl.multiple_of(b * BLOCK, BLOCK), BLOCK)
         lu = lu_col[span, :]
@@ -179,152 +178,172 @@
         return carry
 
     lax.fori_loop(0, blocks, sweep_two, 0)
-    z_stats[ring, pl.ds(row_tiles, 1), :] = jnp.sum(z_part, axis=0, keepdims=True)
     col_lse_rows = []
     hits_rows = []
     for t in range(tiles):
         total = jnp.sum(col_sum[t], axis=0, keepdims=True)
         col_lse_rows.append(col_max[t, 0:1, :] + jnp.log(total))
         hits_rows.append(jnp.sum(hits_acc[t], axis=0, keepdims=True))
-    c_stats[0] = jnp.concatenate(col_lse_rows + hits_rows, axis=0)
-
-    pl.semaphore_wait(barrier, rings - 1 + chips - 1 + 1)
-    core_stat = remote(c_stats.at[0], c_stats.at[1], c_sems.at[0], c_sems.at[1], (twin, ring))
-    core_stat.start()
+    p_stats[mine] = jnp.concatenate(col_lse_rows + hits_rows, axis=0)
+
+    pl.semaphore_wait(barrier, rings - 1 + 2 * chips - 1)
     for step in z_steps:
         remote(
             z_stats.at[ring], z_stats.at[ring], z_sems.at[0], z_sems.at[1], z_peer(step)
         ).start()
-    core_stat.wait()
-    one, two = c_stats[0], c_stats[1]
-    p_stats[chip, 0:tiles, :] = merged_lse(jnp.stack([one[:tiles], two[:tiles]]))
-    p_stats[chip, tiles : 2 * tiles, :] = one[tiles:] + two[tiles:]
-    for step in chip_steps:
+    for step in row_steps:
         remote(
-            p_stats.at[chip], p_stats.at[chip], p_sems.at[0], p_sems.at[1], chip_peer(step)
+            p_stats.at[mine], p_stats.at[mine], p_sems.at[0], p_sems.at[1], row_peer(step)
         ).start()
     wait_bytes(z_stats.at[pl.ds(0, rings - 1)], z_sems.at[1])
-    user_stats = z_stats[...]
-    row_lse = merged_lse(user_stats[:, :row_tiles])
+    row_lse = merged_lse(z_stats[...])
     for k in range(row_tiles):
         row_col[pl.ds(k * LANES, LANES), :] = columns_of(row_lse[k : k + 1, :])
-    user_loss = jnp.sum(row_lse + log_user, axis=0, keepdims=True) - jnp.sum(
-        user_stats[:, row_tiles : row_tiles + 1], axis=0
-    )
-    wait_bytes(p_stats.at[pl.ds(0, chips - 1)], p_sems.at[1])
+    user_loss = jnp.sum(row_lse + log_user, axis=0, keepdims=True)
+    match_loss = jnp.sum(z_part, axis=0, keepdims=True)
+    loss_rows = jnp.concatenate([user_loss, match_loss, jnp.zeros((6, LANES), F32)], axis=0)
+    wait_bytes(p_stats.at[pl.ds(0, 2 * chips - 1)], p_sems.at[1])
     item_stats = p_stats[...]
     col_lse = merged_lse(item_stats[:, :tiles])
     pos_hits = jnp.sum(item_stats[:, tiles:], axis=0)
-    z_loss[ring] = jnp.broadcast_to(
-        jnp.sum(pos_hits * col_lse, axis=0, keepdims=True), (8, LANES)
-    )
-
-    group = rings // WINDOW
-    strip = BLOCK // group
-    place = ring // WINDOW
-    halves = (pl.ds(0, BLOCK // 2), pl.ds(BLOCK // 2, BLOCK // 2))
-
-    def block_at(index):
-        return pl.ds(pl.multiple_of(index % WINDOW * BLOCK, BLOCK), BLOCK)
-
-    def half_at(index, k):
-        start = index % WINDOW * BLOCK + k * (BLOCK // 2)
-        return pl.ds(pl.multiple_of(start, BLOCK // 2), BLOCK // 2)
-
-    def strip_at(index, k):
-        start = index % WINDOW * BLOCK + k % group * strip
+    item_loss = jnp.sum(pos_hits * col_lse, axis=0, keepdims=True)
+
+    strip = rows_here // rings
+    per_block = BLOCK // strip
+    direct = rings // 8
+    hub = 2 * direct + 1
+    covers = [c for c in range(-direct, direct + 1) if c != 0 and hub + c < rings // 2]
+    far = rings // 2 - hub
+    order = [(direct + 1 + j) % rings for j in range(rings)]
+    signs = (1, -1)
+
+    def strip_at(offset):
+        start = (ring + offset + rings) % rings * strip
         return pl.ds(pl.multiple_of(start, strip), strip)
 
-    def user_block(index):
-        span = block_at(index)
-        lu = lu_col[span, :]
-        pos = pos_col[span, :]
-        row = row_col[span, :]
-        for t in range(tiles):
-            s = scores[span, t * LANES : (t + 1) * LANES]
-            value = jnp.exp(s - log_item[t : t + 1, :] - row) + pos_hits[t : t + 1, :] * jnp.exp(
-                s - lu - col_lse[t : t + 1, :]
-            )
-            match = pos == lane + float(t * LANES)
-            value = value - jnp.where(match, 2.0, 0.0)
-            at = (t % half_tiles) * LANES
-            coupling[t // half_tiles, span, at : at + LANES] = value.astype(jnp.bfloat16)
+    def part_at(offset):
+        return pl.ds(order.index(offset % rings) * strip, strip)
+
+    def z_at(offset):
+        return z_peer(offset % rings)
+
+    def halves(index):
+        return pl.ds(index * (strip // 2), strip // 2)
+
+    strip_lane = lane[:strip, :]
+
+    def user_block(b):
+        for j in range(b * per_block, (b + 1) * per_block):
+            source = strip_at(order[j])
+            target = pl.ds(j * strip, strip)
+            users[target, :] = user_ref[source, :]
+            lu = lu_col[source, :]
+            pos = pos_col[source, :]
+            row = row_col[source, :]
+            for t in range(tiles):
+                s = scores[source, t * LANES : (t + 1) * LANES]
+                value = jnp.exp(s - log_item[t : t + 1, :] - row) + pos_hits[
+                    t : t + 1, :
+                ] * jnp.exp(s - lu - col_lse[t : t + 1, :])
+                match = pos == strip_lane + float(t * LANES)
+                value = value - jnp.where(match, 2.0, 0.0)
+                at = (t % half_tiles) * LANES
+                coupling[t // half_tiles, target, at : at + LANES] = value.astype(jnp.bfloat16)
+        span = pl.ds(b * BLOCK, BLOCK)
         part[span, :] = 2.0 * (
             jnp.dot(coupling[0, span, :], item_ref[:half_cols, :], preferred_element_type=F32)
             + jnp.dot(coupling[1, span, :], item_ref[half_cols:, :], preferred_element_type=F32)
         )
 
-    near = ((1, 0), (rings - 1, 1))
-
-    def window_send(step, slot):
-        for k in range(2):
-            remote(
-                part.at[half_at(ring + step, k), :],
-                window_in.at[slot, halves[k], :],
+    leaving = {}
+    hub_half = pl.ds(len(covers) * strip, strip // 2)
+    for index, sign in enumerate(signs):
+        for slot, c in enumerate(covers):
+            leaving.setdefault(-sign * (hub + c) % rings, []).append(
+                (
+                    part.at[part_at(-sign * (hub + c)), :],
+                    hub_in.at[index, pl.ds(slot * strip, strip), :],
+                    w_sems.at[0],
+                    w_sems.at[1 + index],
+                    z_at(-sign * c),
+                )
+            )
+        leaving.setdefault(rings // 2, []).append(
+            (
+                part.at[pl.ds(part_at(rings // 2).start + index * (strip // 2), strip // 2), :],
+                hub_in.at[index, hub_half, :],
                 w_sems.at[0],
-                w_sems.at[1],
-                z_peer(step),
-            ).start()
-
-    for step, slot in near:
-        user_block(ring + step)
-        window_send(step, slot)
-    user_block(ring + 2)
-    for k, step in enumerate((2, rings - 2)):
+                w_sems.at[1 + index],
+                z_at(-sign * far),
+            )
+        )
+        for step in range(1, direct + 1):
+            leaving.setdefault(-sign * step % rings, []).append(
+                (
+                    part.at[part_at(-sign * step), :],
+                    near_in.at[index * direct + step - 1],
+                    w_sems.at[3],
+                    w_sems.at[4],
+                    z_at(-sign * step),
+                )
+            )
+
+    for b in range(blocks):
+        user_block(b)
+        for j in range(b * per_block, (b + 1) * per_block):
+            for copy in leaving.get(order[j], ()):
+                remote(*copy).start()
+
+    def hub_sum(index):
+        sign = signs[index]
+        wait_bytes(hub_in.at[index], w_sems.at[1 + index])
+        span = part_at(-sign * hub)
+        total = part[span, :]
+        for slot in range(len(covers)):
+            total = total + hub_in[index, slot * strip : (slot + 1) * strip, :]
+        part[span, :] = total
+        half = pl.ds(span.start + index * (strip // 2), strip // 2)
+        part[half, :] += hub_in[index, hub_half, :]
         remote(
-            part.at[half_at(ring + 2, k), :],
-            window_in.at[2, halves[k], :],
-            w_sems.at[0],
-            w_sems.at[1],
-            z_peer(step),
+            part.at[span, :],
+            near_in.at[2 * direct + index],
+            w_sems.at[3],
+            w_sems.at[4],
+            z_at(-sign * hub),
         ).start()
-    user_block(ring)
-
-    def stride_send():
-        wait_bytes(window_in, w_sems.at[1])
-        span = block_at(ring)
-        part[span, :] += window_in[0] + window_in[1] + window_in[2]
-        for k in range(1, group):
-            remote(
-                part.at[strip_at(ring, place + k), :],
-                stride_in.at[k - 1],
-                w_sems.at[2],
-                w_sems.at[3],
-                z_peer(k * WINDOW),
-            ).start()
-
-    def spread(index):
-        here = ug_ref.at[strip_at(ring, index), :]
-        for step in (1, rings - 1):
-            remote(here, here, w_sems.at[4], w_sems.at[5], z_peer(step)).start()
-        low = index % group < group // 2
-        far = jnp.where(low, 2, rings - 2)
-        remote(here, here, w_sems.at[4], w_sems.at[5], z_peer(far)).start()
-
-    def stride_sum():
-        wait_bytes(stride_in, w_sems.at[3])
-        span = strip_at(ring, place)
-        total = part[span, :]
-        for k in range(group - 1):
-            total = total + stride_in[k]
+
+    def own_sum():
+        wait_bytes(near_in, w_sems.at[4])
+        total = part[part_at(0), :]
+        for slot in range(2 * direct + 2):
+            total = total + near_in[slot]
+        span = strip_at(0)
         ug_ref[span, :] = total
         here = ug_ref.at[span, :]
-        for k in range(1, group):
-            remote(here, here, w_sems.at[6], g_sems.at[k - 1], z_peer(k * WINDOW)).start()
-        spread(place)
-
-    def spread_on(k):
-        index = place + group - k
-        wait_bytes(ug_ref.at[strip_at(ring, index), :], g_sems.at[k - 1])
-        spread(index)
+        for index, sign in enumerate(signs):
+            remote(here, here, w_sems.at[5], g_sems.at[index], z_at(sign * hub)).start()
+        for step in range(1, direct + 1):
+            for sign in signs:
+                remote(here, here, w_sems.at[5], w_sems.at[6], z_at(sign * step)).start()
+
+    def hub_spread(index):
+        sign = signs[index]
+        start = (ring - sign * hub + rings) % rings * strip
+        here = ug_ref.at[pl.ds(pl.multiple_of(start, strip), strip), :]
+        wait_bytes(here, g_sems.at[index])
+        half_start = pl.multiple_of(start + index * (strip // 2), strip // 2)
+        half = ug_ref.at[pl.ds(half_start, strip // 2), :]
+        remote(half, half, w_sems.at[5], w_sems.at[6], z_at(sign * far)).start()
+        for c in sorted(covers, key=lambda c: -abs(c)):
+            remote(here, here, w_sems.at[5], w_sems.at[6], z_at(sign * c)).start()
 
     def gather_end():
-        wait_bytes(ug_ref.at[pl.ds(0, (WINDOW - 1) * BLOCK), :], w_sems.at[5])
+        wait_bytes(ug_ref.at[pl.ds(0, (rings - 3) * strip), :], w_sems.at[6])
 
     def item_part(which):
         items[which, :half_cols, :] = 2.0 * lax.dot_general(
             coupling[which],
-            user_ref[...],
+            users[...],
             (((0,), (0,)), ((), ())),
             preferred_element_type=F32,
         )
@@ -333,7 +352,7 @@
 
     def core_send():
         item_part(other)
-        items[other, half_cols:, :LANES] = jnp.broadcast_to(user_loss, (8, LANES))
+        items[other, half_cols:, :LANES] = loss_rows
         items[other, half_cols:, LANES:] = jnp.zeros((8, width - LANES), F32)
         for k in range(CORE_PARTS):
             extra = 8 if k == CORE_PARTS - 1 else 0
@@ -346,15 +365,9 @@
                 (twin, ring),
             ).start()
 
-    def loss_send():
-        for step in z_steps:
-            remote(
-                z_loss.at[ring], z_loss.at[ring], l_sems.at[0], l_sems.at[1], z_peer(step)
-            ).start()
-
     def plane_send():
         wait_bytes(core_in, x_sems.at[1])
-        pair_loss = core_in[half_cols:, :LANES] + user_loss
+        pair_loss = core_in[half_cols:, :LANES] + loss_rows
 
         def pack(k, carry):
             span = pl.ds(pl.multiple_of(k * piece, piece), piece)
@@ -390,6 +403,13 @@
                 here, here, x_sems.at[4], back_sems.at[step - 1], chip_peer(step)
             ).start()
         remote(here, here, x_sems.at[5], x_sems.at[6], (twin, ring)).start()
+        z_loss[ring] = jnp.broadcast_to(
+            item_loss - total[piece + 1 : piece + 2, :LANES], (8, LANES)
+        )
+        for step in z_steps:
+            remote(
+                z_loss.at[ring], z_loss.at[ring], l_sems.at[0], l_sems.at[1], z_peer(step)
+            ).start()
         return total[piece : piece + 1, :LANES]
 
     def forward(step):
@@ -408,25 +428,25 @@
 
     core_send()
     item_part(core)
-    loss_send()
     plane_send()
-    stride_send()
-    stride_sum()
-    loss_end(plane_sum())
-    for k in sorted(range(1, group), key=lambda k: min(k, group - k)):
-        spread_on(k)
+    hub_sum(0)
+    hub_sum(1)
+    own_sum()
+    users_total = plane_sum()
+    hub_spread(0)
+    hub_spread(1)
     for step in chip_steps:
         forward(step)
+    loss_end(users_total)
     gather_end()
     wait_bytes(ig_ref.at[pl.ds(0, half_cols), :], x_sems.at[6])
 
     wait_bytes(z_stats.at[pl.ds(0, rings - 1)], z_sems.at[0])
-    wait_bytes(p_stats.at[pl.ds(0, chips - 1)], p_sems.at[0])
+    wait_bytes(p_stats.at[pl.ds(0, 2 * chips - 1)], p_sems.at[0])
     wait_bytes(z_loss.at[pl.ds(0, rings - 1)], l_sems.at[0])
-    wait_bytes(window_in, w_sems.at[0])
-    wait_bytes(stride_in, w_sems.at[2])
-    wait_bytes(ug_ref.at[pl.ds(0, (WINDOW - 1) * BLOCK), :], w_sems.at[4])
-    wait_bytes(stride_in, w_sems.at[6])
+    wait_bytes(hub_in, w_sems.at[0])
+    wait_bytes(near_in, w_sems.at[3])
+    wait_bytes(ug_ref.at[pl.ds(0, (rings - 1) * strip), :], w_sems.at[5])
     wait_bytes(core_in, x_sems.at[0])
     wait_bytes(plane_in.at[pl.ds(0, chips - 1)], x_sems.at[2])
     wait_bytes(ig_ref.at[others, :], x_sems.at[4])
@@ -437,7 +457,9 @@
     rows, width = user_embed.shape
     cols = item_embed.shape[0]
     tiles = cols // LANES
-    group = rings // WINDOW
+    strip = rows // rings
+    direct = rings // 8
+    hub_rows = (2 * direct if rings > 8 else 1) * strip + strip // 2
     piece = cols // 2 // chips
     vmem = pl.BlockSpec(memory_space=pltpu.VMEM)
     dma = pltpu.SemaphoreType.DMA
@@ -453,6 +475,7 @@
         scratch_shapes=[
             pltpu.VMEM((rows, width), user_embed.dtype),
             pltpu.VMEM((cols, width), item_embed.dtype),
+            pltpu.VMEM((rows, width), user_embed.dtype),
             pltpu.VMEM((rows, cols), F32),
             pltpu.VMEM((2, rows, cols // 2), jnp.bfloat16),
             pltpu.VMEM((rows, width), F32),
@@ -464,21 +487,19 @@
             pltpu.VMEM((tiles, 8, LANES), F32),
             pltpu.VMEM((tiles, 8, LANES), F32),
             pltpu.VMEM((tiles, 8, LANES), F32),
+            pltpu.VMEM((rings, rows // LANES, LANES), F32),
+            pltpu.VMEM((2 * chips, 2 * tiles, LANES), F32),
             pltpu.VMEM((rings, 8, LANES), F32),
-            pltpu.VMEM((2, 2 * tiles, LANES), F32),
-            pltpu.VMEM((chips, 2 * tiles, LANES), F32),
-            pltpu.VMEM((rings, 8, LANES), F32),
-            pltpu.VMEM((WINDOW - 1, BLOCK, width), F32),
-            pltpu.VMEM((group - 1, BLOCK // group, width), F32),
+            pltpu.VMEM((2, hub_rows, width), F32),
+            pltpu.VMEM((2 * direct + 2, strip, width), F32),
             pltpu.VMEM((cols // 2 + 8, width), F32),
             pltpu.VMEM((chips, piece + 8, width), F32),
             pltpu.VMEM((chips, piece + 8, width), F32),
             dma((2,)),
             dma((2,)),
             dma((2,)),
+            dma((7,)),
             dma((2,)),
-            dma((7,)),
-            dma((group - 1,)),
             dma((8,)),
             dma((chips - 1,)),
             dma((2,)),

time: 64.1 us -> 59.6 us (0.930)
  the two profiles are of different devices: /device:TPU:70 before, /device:TPU:1 now
where the time goes in v3:
time: 59.6 us; the launch traced here: 59.4 us
  Pallas kernels  54 us (91%)
  local copies, waits for them, and re-layouts  2.93 us (5%)
  between operations  2.41 us (4%)
    pallas_call x1, Pallas kernels, per_device(): pl.pallas_call(functools.partial(kernel, total_users, chips, rings), out_...  54 us
    unnamed x4, local copies, waits for them, and re-layouts  2.93 us

profile of v3, /device:TPU:1, one launch (start us, length us, event | category | flops | bytes accessed | tf_op | source)
XLA Modules:
  0.0 59.4 jit_solution(17902245748113885649)
XLA Ops:
  0.6 54.0 %two_sided.1 = (f32[512,256]{1,0:T(8,128)}, f32[1024,256]{1,0:T(8,128)}, f32[1,1]{1,0:T(1,128)}) custom-call(bf16[512,256]{1,0:T(8,128)(2,1)} %user_hbm.1, bf16[1024,256]{1,0:T(8,128)(2,1)} %item_hbm.1, s32[4,128]{1,0:T(4,128)} %bitcast.5, s32[4,128]{1,0:T(4,128)} %bitcast.6, s32[8,128]{1,0:T(8,128)} %bitcast.4), custom_call_target="tpu_custom_call" | custom-call | tf_op jit(solution)/shard_map/two_sided/pallas_call | solution.py:466
  54.7 0.0 copy-start
  54.7 2.0 %copy.11 = f32[512,256]{1,0:T(8,128)} copy(f32[512,256]{1,0:T(8,128)} %get-tuple-element.12) | data formatting | bytes 1048576
  56.6 0.0 copy-done
  56.6 1.0 %copy.12 = f32[1024,256]{1,0:T(8,128)} copy(f32[1024,256]{1,0:T(8,128)S(1)} %copy-done) | data formatting | bytes 2097152
Async XLA Ops:
  54.7 2.0 %copy-start = (f32[1024,256]{1,0:T(8,128)S(1)}, f32[1024,256]{1,0:T(8,128)}, u32[]{:S(2)}) copy-start(f32[1024,256]{1,0:T(8,128)} %get-tuple-element.13) | copy-start | bytes 3145732

commit v4 on v3

--- a/solution.py
+++ b/solution.py
@@ -43,6 +43,8 @@
     item_ref,
     users,
     scores,
+    row_exp,
+    col_exp,
     coupling,
     part,
     items,
@@ -135,7 +137,17 @@
     hits_acc[...] = jnp.zeros(hits_acc.shape, F32)
     lane = lax.broadcasted_iota(jnp.int32, (BLOCK, LANES), 1).astype(F32)
 
-    def sweep_one(b, z_part):
+    def count_hits(b, carry):
+        span = pl.ds(pl.multiple_of(b * BLOCK, BLOCK), BLOCK)
+        pos = pos_col[span, :]
+        for t in range(tiles):
+            match = pos == lane + float(t * LANES)
+            hits_acc[t] += jnp.sum(fold(jnp.where(match, 1.0, 0.0)), axis=0)
+        return carry
+
+    lax.fori_loop(0, blocks, count_hits, 0)
+
+    def sweep_one(b, carry):
         span = pl.ds(pl.multiple_of(b * BLOCK, BLOCK), BLOCK)
         scores[span, :] = 2.0 * lax.dot_general(
             user_ref[span, :],
@@ -144,22 +156,18 @@
             preferred_element_type=F32,
         )
         lu = lu_col[span, :]
-        pos = pos_col[span, :]
         top = None
         for t in range(tiles):
             s = scores[span, t * LANES : (t + 1) * LANES]
             shifted = s - log_item[t : t + 1, :]
             top = shifted if top is None else jnp.maximum(top, shifted)
             col_max[t] = jnp.maximum(col_max[t], jnp.max(fold(s - lu), axis=0))
-            match = pos == lane + float(t * LANES)
-            hits_acc[t] += jnp.sum(fold(jnp.where(match, 1.0, 0.0)), axis=0)
-            z_part = z_part + jnp.sum(fold(jnp.where(match, s + shifted, 0.0)), axis=0)
         row_col[span, :] = jnp.broadcast_to(jnp.max(top, axis=1, keepdims=True), (BLOCK, LANES))
-        return z_part
+        return carry
 
     item_in.wait()
     user_in.wait()
-    z_part = lax.fori_loop(0, blocks, sweep_one, jnp.zeros((8, LANES), F32))
+    lax.fori_loop(0, blocks, sweep_one, 0)
     for t in range(tiles):
         col_max[t] = jnp.broadcast_to(jnp.max(col_max[t], axis=0, keepdims=True), (8, LANES))
 
@@ -170,9 +178,12 @@
         total = jnp.zeros((BLOCK, LANES), F32)
         for t in range(tiles):
             s = scores[span, t * LANES : (t + 1) * LANES]
-            total = total + jnp.exp(s - log_item[t : t + 1, :] - row_max)
-            col = jnp.exp(fold(s - lu) - col_max[t][None])
-            col_sum[t] += jnp.sum(col, axis=0)
+            row = jnp.exp(s - log_item[t : t + 1, :] - row_max)
+            row_exp[span, t * LANES : (t + 1) * LANES] = row
+            total = total + row
+            col = jnp.exp(s - lu - col_max[t, 0:1, :])
+            col_exp[span, t * LANES : (t + 1) * LANES] = col
+            col_sum[t] += jnp.sum(fold(col), axis=0)
         lse = row_max + jnp.log(jnp.sum(total, axis=1, keepdims=True))
         z_stats[ring, pl.ds(b, 1), :] = jnp.transpose(lse)[0:1, :]
         return carry
@@ -195,18 +206,34 @@
         remote(
             p_stats.at[mine], p_stats.at[mine], p_sems.at[0], p_sems.at[1], row_peer(step)
         ).start()
+
+    def match_scores(b, so_far):
+        span = pl.ds(pl.multiple_of(b * BLOCK, BLOCK), BLOCK)
+        pos = pos_col[span, :]
+        for t in range(tiles):
+            s = scores[span, t * LANES : (t + 1) * LANES]
+            match = pos == lane + float(t * LANES)
+            value = jnp.where(match, s + s - log_item[t : t + 1, :], 0.0)
+            so_far = so_far + jnp.sum(fold(value), axis=0)
+        return so_far
+
+    z_part = lax.fori_loop(0, blocks, match_scores, jnp.zeros((8, LANES), F32))
+    match_loss = jnp.sum(z_part, axis=0, keepdims=True)
+
     wait_bytes(z_stats.at[pl.ds(0, rings - 1)], z_sems.at[1])
     row_lse = merged_lse(z_stats[...])
     for k in range(row_tiles):
-        row_col[pl.ds(k * LANES, LANES), :] = columns_of(row_lse[k : k + 1, :])
+        span = pl.ds(k * LANES, LANES)
+        row_col[span, :] = jnp.exp(row_col[span, :] - columns_of(row_lse[k : k + 1, :]))
     user_loss = jnp.sum(row_lse + log_user, axis=0, keepdims=True)
-    match_loss = jnp.sum(z_part, axis=0, keepdims=True)
     loss_rows = jnp.concatenate([user_loss, match_loss, jnp.zeros((6, LANES), F32)], axis=0)
     wait_bytes(p_stats.at[pl.ds(0, 2 * chips - 1)], p_sems.at[1])
     item_stats = p_stats[...]
     col_lse = merged_lse(item_stats[:, :tiles])
     pos_hits = jnp.sum(item_stats[:, tiles:], axis=0)
     item_loss = jnp.sum(pos_hits * col_lse, axis=0, keepdims=True)
+    col_top = jnp.concatenate([col_max[t, 0:1, :] for t in range(tiles)], axis=0)
+    col_scale = pos_hits * jnp.exp(col_top - col_lse)
 
     strip = rows_here // rings
     per_block = BLOCK // strip
@@ -237,14 +264,11 @@
             source = strip_at(order[j])
             target = pl.ds(j * strip, strip)
             users[target, :] = user_ref[source, :]
-            lu = lu_col[source, :]
             pos = pos_col[source, :]
             row = row_col[source, :]
             for t in range(tiles):
-                s = scores[source, t * LANES : (t + 1) * LANES]
-                value = jnp.exp(s - log_item[t : t + 1, :] - row) + pos_hits[
-                    t : t + 1, :
-                ] * jnp.exp(s - lu - col_lse[t : t + 1, :])
+                here = slice(t * LANES, (t + 1) * LANES)
+                value = row_exp[source, here] * row + col_exp[source, here] * col_scale[t : t + 1, :]
                 match = pos == strip_lane + float(t * LANES)
                 value = value - jnp.where(match, 2.0, 0.0)
                 at = (t % half_tiles) * LANES
@@ -403,14 +427,14 @@
                 here, here, x_sems.at[4], back_sems.at[step - 1], chip_peer(step)
             ).start()
         remote(here, here, x_sems.at[5], x_sems.at[6], (twin, ring)).start()
-        z_loss[ring] = jnp.broadcast_to(
-            item_loss - total[piece + 1 : piece + 2, :LANES], (8, LANES)
-        )
+        return total[piece : piece + 8, :LANES]
+
+    def loss_send(total):
+        z_loss[ring] = jnp.broadcast_to(item_loss - total[1:2, :], (8, LANES))
         for step in z_steps:
             remote(
                 z_loss.at[ring], z_loss.at[ring], l_sems.at[0], l_sems.at[1], z_peer(step)
             ).start()
-        return total[piece : piece + 1, :LANES]
 
     def forward(step):
         here = ig_ref.at[piece_at(core, chip + chips - step), :]
@@ -428,16 +452,17 @@
 
     core_send()
     item_part(core)
-    plane_send()
     hub_sum(0)
     hub_sum(1)
+    plane_send()
     own_sum()
-    users_total = plane_sum()
+    plane_total = plane_sum()
     hub_spread(0)
     hub_spread(1)
+    loss_send(plane_total)
     for step in chip_steps:
         forward(step)
-    loss_end(users_total)
+    loss_end(plane_total[0:1, :])
     gather_end()
     wait_bytes(ig_ref.at[pl.ds(0, half_cols), :], x_sems.at[6])
 
@@ -476,6 +501,8 @@
             pltpu.VMEM((rows, width), user_embed.dtype),
             pltpu.VMEM((cols, width), item_embed.dtype),
             pltpu.VMEM((rows, width), user_embed.dtype),
+            pltpu.VMEM((rows, cols), F32),
+            pltpu.VMEM((rows, cols), F32),
             pltpu.VMEM((rows, cols), F32),
             pltpu.VMEM((2, rows, cols // 2), jnp.bfloat16),
             pltpu.VMEM((rows, width), F32),

time: 59.6 us -> 63 us (1.057)
  the two profiles are of different devices: /device:TPU:1 before, /device:TPU:32 now
where the time goes in v4:
time: 63 us; the launch traced here: 62.8 us
  Pallas kernels  57.5 us (91%)
  local copies, waits for them, and re-layouts  2.93 us (5%)
  between operations  2.41 us (4%)
    pallas_call x1, Pallas kernels, per_device(): pl.pallas_call(functools.partial(kernel, total_users, chips, rings), out_...  57.5 us
    unnamed x4, local copies, waits for them, and re-layouts  2.93 us

profile of v4, /device:TPU:32, one launch (start us, length us, event | category | flops | bytes accessed | tf_op | source)
XLA Modules:
  0.0 62.8 jit_solution(12422913904940155519)
XLA Ops:
  0.6 57.5 %two_sided.1 = (f32[512,256]{1,0:T(8,128)}, f32[1024,256]{1,0:T(8,128)}, f32[1,1]{1,0:T(1,128)}) custom-call(bf16[512,256]{1,0:T(8,128)(2,1)} %user_hbm.1, bf16[1024,256]{1,0:T(8,128)(2,1)} %item_hbm.1, s32[4,128]{1,0:T(4,128)} %bitcast.5, s32[4,128]{1,0:T(4,128)} %bitcast.6, s32[8,128]{1,0:T(8,128)} %bitcast.4), custom_call_target="tpu_custom_call" | custom-call | tf_op jit(solution)/shard_map/two_sided/pallas_call | solution.py:491
  58.1 0.0 copy-start
  58.1 2.0 %copy.11 = f32[512,256]{1,0:T(8,128)} copy(f32[512,256]{1,0:T(8,128)} %get-tuple-element.12) | data formatting | bytes 1048576
  60.1 0.0 copy-done
  60.1 1.0 %copy.12 = f32[1024,256]{1,0:T(8,128)} copy(f32[1024,256]{1,0:T(8,128)S(1)} %copy-done) | data formatting | bytes 2097152
Async XLA Ops:
  58.1 2.0 %copy-start = (f32[1024,256]{1,0:T(8,128)S(1)}, f32[1024,256]{1,0:T(8,128)}, u32[]{:S(2)}) copy-start(f32[1024,256]{1,0:T(8,128)} %get-tuple-element.13) | copy-start | bytes 3145732

commit v5 on v3

--- a/solution.py
+++ b/solution.py
@@ -36,13 +36,17 @@
     pos_ref,
     ucnt_ref,
     icnt_ref,
+    ug_hbm,
+    ig_hbm,
+    loss_ref,
     ug_ref,
     ig_ref,
-    loss_ref,
     user_ref,
     item_ref,
     users,
     scores,
+    row_exp,
+    col_exp,
     coupling,
     part,
     items,
@@ -69,6 +73,7 @@
     x_sems,
     back_sems,
     in_sems,
+    out_sems,
 ):
     rows_here, width = user_ref.shape
     cols_here = item_ref.shape[0]
@@ -170,9 +175,12 @@
         total = jnp.zeros((BLOCK, LANES), F32)
         for t in range(tiles):
             s = scores[span, t * LANES : (t + 1) * LANES]
-            total = total + jnp.exp(s - log_item[t : t + 1, :] - row_max)
-            col = jnp.exp(fold(s - lu) - col_max[t][None])
-            col_sum[t] += jnp.sum(col, axis=0)
+            row = jnp.exp(s - log_item[t : t + 1, :] - row_max)
+            row_exp[span, t * LANES : (t + 1) * LANES] = row
+            total = total + row
+            col = jnp.exp(s - lu - col_max[t, 0:1, :])
+            col_exp[span, t * LANES : (t + 1) * LANES] = col
+            col_sum[t] += jnp.sum(fold(col), axis=0)
         lse = row_max + jnp.log(jnp.sum(total, axis=1, keepdims=True))
         z_stats[ring, pl.ds(b, 1), :] = jnp.transpose(lse)[0:1, :]
         return carry
@@ -198,7 +206,8 @@
     wait_bytes(z_stats.at[pl.ds(0, rings - 1)], z_sems.at[1])
     row_lse = merged_lse(z_stats[...])
     for k in range(row_tiles):
-        row_col[pl.ds(k * LANES, LANES), :] = columns_of(row_lse[k : k + 1, :])
+        span = pl.ds(k * LANES, LANES)
+        row_col[span, :] = jnp.exp(row_col[span, :] - columns_of(row_lse[k : k + 1, :]))
     user_loss = jnp.sum(row_lse + log_user, axis=0, keepdims=True)
     match_loss = jnp.sum(z_part, axis=0, keepdims=True)
     loss_rows = jnp.concatenate([user_loss, match_loss, jnp.zeros((6, LANES), F32)], axis=0)
@@ -207,6 +216,8 @@
     col_lse = merged_lse(item_stats[:, :tiles])
     pos_hits = jnp.sum(item_stats[:, tiles:], axis=0)
     item_loss = jnp.sum(pos_hits * col_lse, axis=0, keepdims=True)
+    col_top = jnp.concatenate([col_max[t, 0:1, :] for t in range(tiles)], axis=0)
+    col_scale = pos_hits * jnp.exp(col_top - col_lse)
 
     strip = rows_here // rings
     per_block = BLOCK // strip
@@ -237,14 +248,11 @@
             source = strip_at(order[j])
             target = pl.ds(j * strip, strip)
             users[target, :] = user_ref[source, :]
-            lu = lu_col[source, :]
             pos = pos_col[source, :]
             row = row_col[source, :]
             for t in range(tiles):
-                s = scores[source, t * LANES : (t + 1) * LANES]
-                value = jnp.exp(s - log_item[t : t + 1, :] - row) + pos_hits[
-                    t : t + 1, :
-                ] * jnp.exp(s - lu - col_lse[t : t + 1, :])
+                here = slice(t * LANES, (t + 1) * LANES)
+                value = row_exp[source, here] * row + col_exp[source, here] * col_scale[t : t + 1, :]
                 match = pos == strip_lane + float(t * LANES)
                 value = value - jnp.where(match, 2.0, 0.0)
                 at = (t % half_tiles) * LANES
@@ -438,8 +446,16 @@
     for step in chip_steps:
         forward(step)
     loss_end(users_total)
+    def half_out(which):
+        span = pl.ds(pl.multiple_of(which * half_cols, half_cols), half_cols)
+        return pltpu.make_async_copy(ig_ref.at[span, :], ig_hbm.at[span, :], out_sems.at[which])
+
+    half_out(core).start()
     gather_end()
+    user_out = pltpu.make_async_copy(ug_ref, ug_hbm, out_sems.at[2])
+    user_out.start()
     wait_bytes(ig_ref.at[pl.ds(0, half_cols), :], x_sems.at[6])
+    half_out(other).start()
 
     wait_bytes(z_stats.at[pl.ds(0, rings - 1)], z_sems.at[0])
     wait_bytes(p_stats.at[pl.ds(0, 2 * chips - 1)], p_sems.at[0])
@@ -451,6 +467,35 @@
     wait_bytes(plane_in.at[pl.ds(0, chips - 1)], x_sems.at[2])
     wait_bytes(ig_ref.at[others, :], x_sems.at[4])
     wait_bytes(ig_ref.at[pl.ds(0, half_cols), :], x_sems.at[5])
+    half_out(core).wait()
+    user_out.wait()
+    half_out(other).wait()
+
+
+def copy_out(ug_in, ig_in, ug_out, ig_out, ug_here, ig_here, sems):
+    loads = []
+    stores = []
+    for source, here, target, count in (
+        (ug_in, ug_here, ug_out, 2),
+        (ig_in, ig_here, ig_out, 4),
+    ):
+        rows = source.shape[0] // count
+        for k in range(count):
+            span = pl.ds(k * rows, rows)
+            slot = len(loads)
+            loads.append(
+                pltpu.make_async_copy(source.at[span, :], here.at[span, :], sems.at[0, slot])
+            )
+            stores.append(
+                pltpu.make_async_copy(here.at[span, :], target.at[span, :], sems.at[1, slot])
+            )
+    for load in loads:
+        load.start()
+    for load, store in zip(loads, stores):
+        load.wait()
+        store.start()
+    for store in stores:
+        store.wait()
 
 
 def per_device(total_users, chips, rings, user_embed, item_embed, positive, user_count, item_count):
@@ -462,6 +507,7 @@
     hub_rows = (2 * direct if rings > 8 else 1) * strip + strip // 2
     piece = cols // 2 // chips
     vmem = pl.BlockSpec(memory_space=pltpu.VMEM)
+    hbm = pl.BlockSpec(memory_space=pltpu.HBM)
     dma = pltpu.SemaphoreType.DMA
     user_grad, item_grad, loss = pl.pallas_call(
         functools.partial(kernel, total_users, chips, rings),
@@ -470,12 +516,16 @@
             jax.ShapeDtypeStruct((cols, width), F32),
             jax.ShapeDtypeStruct((1, 1), F32),
         ),
-        in_specs=[pl.BlockSpec(memory_space=pltpu.HBM)] * 2 + [vmem] * 3,
-        out_specs=(vmem, vmem, pl.BlockSpec(memory_space=pltpu.SMEM)),
+        in_specs=[hbm] * 2 + [vmem] * 3,
+        out_specs=(hbm, hbm, pl.BlockSpec(memory_space=pltpu.SMEM)),
         scratch_shapes=[
+            pltpu.VMEM((rows, width), F32),
+            pltpu.VMEM((cols, width), F32),
             pltpu.VMEM((rows, width), user_embed.dtype),
             pltpu.VMEM((cols, width), item_embed.dtype),
             pltpu.VMEM((rows, width), user_embed.dtype),
+            pltpu.VMEM((rows, cols), F32),
+            pltpu.VMEM((rows, cols), F32),
             pltpu.VMEM((rows, cols), F32),
             pltpu.VMEM((2, rows, cols // 2), jnp.bfloat16),
             pltpu.VMEM((rows, width), F32),
@@ -503,6 +553,7 @@
             dma((8,)),
             dma((chips - 1,)),
             dma((2,)),
+            dma((3,)),
         ],
         compiler_params=pltpu.CompilerParams(
             collective_id=0, has_side_effects=True, vmem_limit_bytes=60 * 1024 * 1024
@@ -515,6 +566,22 @@
         user_count.reshape(rows // LANES, LANES),
         item_count.reshape(tiles, LANES),
     )
+    user_grad, item_grad = pl.pallas_call(
+        copy_out,
+        out_shape=(
+            jax.ShapeDtypeStruct((rows, width), F32),
+            jax.ShapeDtypeStruct((cols, width), F32),
+        ),
+        in_specs=[hbm] * 2,
+        out_specs=(hbm, hbm),
+        scratch_shapes=[
+            pltpu.VMEM((rows, width), F32),
+            pltpu.VMEM((cols, width), F32),
+            dma((2, 6)),
+        ],
+        compiler_params=pltpu.CompilerParams(vmem_limit_bytes=60 * 1024 * 1024),
+        name="copy_out",
+    )(user_grad, item_grad)
     return user_grad, item_grad, loss.reshape(())
 
 

time: 59.6 us -> 58.9 us (0.988)
  local copies, waits for them, and re-layouts: 2.93 us -> 0 us
  Pallas kernels: 54 us -> 56.3 us
    unnamed x4 -> x0, local copies, waits for them, and re-layouts: 2.93 us -> none
    pallas_call x0 -> x1, Pallas kernels: none -> 2.19 us  [per_device(): pl.pallas_call(copy_out, out_shape=(jax.ShapeDtypeStruct((rows, width), F...]
where the time goes in v5:
time: 58.9 us; the launch traced here: 58.7 us
  Pallas kernels  56.3 us (96%)
  between operations  2.41 us (4%)
    pallas_call x1, Pallas kernels, per_device(): pl.pallas_call(functools.partial(kernel, total_users, chips, rings), out_...  54.1 us
    pallas_call x1, Pallas kernels, per_device(): pl.pallas_call(copy_out, out_shape=(jax.ShapeDtypeStruct((rows, width), F...  2.19 us

profile of v5, /device:TPU:1, one launch (start us, length us, event | category | flops | bytes accessed | tf_op | source)
XLA Modules:
  0.0 58.7 jit_solution(6894890414287578766)
XLA Ops:
  0.6 54.1 %two_sided.1 = (f32[512,256]{1,0:T(8,128)}, f32[1024,256]{1,0:T(8,128)}, f32[1,1]{1,0:T(1,128)}) custom-call(bf16[512,256]{1,0:T(8,128)(2,1)} %user_hbm.1, bf16[1024,256]{1,0:T(8,128)(2,1)} %item_hbm.1, s32[4,128]{1,0:T(4,128)} %bitcast.5, s32[4,128]{1,0:T(4,128)} %bitcast.6, s32[8,128]{1,0:T(8,128)} %bitcast.4), custom_call_target="tpu_custom_call" | custom-call | tf_op jit(solution)/shard_map/two_sided/pallas_call | solution.py:512
  54.7 2.2 %copy_out.1 = (f32[512,256]{1,0:T(8,128)}, f32[1024,256]{1,0:T(8,128)}) custom-call(f32[512,256]{1,0:T(8,128)} %get-tuple-element.8.ug_in, f32[1024,256]{1,0:T(8,128)} %get-tuple-element.9.ig_in), custom_call_target="tpu_custom_call" | custom-call | tf_op jit(solution)/shard_map/copy_out/pallas_call | solution.py:569

commit v6 on v5

--- a/solution.py
+++ b/solution.py
@@ -11,6 +11,7 @@
 LANES = 128
 BLOCK = 128
 CORE_PARTS = 4
+PARTS = 2
 F32 = jnp.float32
 
 
@@ -65,10 +66,13 @@
     core_in,
     plane_out,
     plane_in,
+    p_loss,
     z_sems,
     p_sems,
     l_sems,
     w_sems,
+    h_sems,
+    n_sems,
     g_sems,
     x_sems,
     back_sems,
@@ -220,7 +224,8 @@
     col_scale = pos_hits * jnp.exp(col_top - col_lse)
 
     strip = rows_here // rings
-    per_block = BLOCK // strip
+    sub = strip // PARTS
+    per_block = BLOCK // sub
     direct = rings // 8
     hub = 2 * direct + 1
     covers = [c for c in range(-direct, direct + 1) if c != 0 and hub + c < rings // 2]
@@ -228,32 +233,31 @@
     order = [(direct + 1 + j) % rings for j in range(rings)]
     signs = (1, -1)
 
-    def strip_at(offset):
-        start = (ring + offset + rings) % rings * strip
-        return pl.ds(pl.multiple_of(start, strip), strip)
-
-    def part_at(offset):
-        return pl.ds(order.index(offset % rings) * strip, strip)
+    def sub_at(offset, h, start=0, size=None):
+        size = sub if size is None else size
+        first = (ring + offset + rings) % rings * strip + h * sub + start
+        return pl.ds(pl.multiple_of(first, 8 if size < 16 else size), size)
+
+    def part_at(offset, h):
+        return pl.ds(h * (rows_here // PARTS) + order.index(offset % rings) * sub, sub)
 
     def z_at(offset):
         return z_peer(offset % rings)
 
-    def halves(index):
-        return pl.ds(index * (strip // 2), strip // 2)
-
-    strip_lane = lane[:strip, :]
+    sub_lane = lane[:sub, :]
 
     def user_block(b):
-        for j in range(b * per_block, (b + 1) * per_block):
-            source = strip_at(order[j])
-            target = pl.ds(j * strip, strip)
+        for k in range(b * per_block, (b + 1) * per_block):
+            h, j = k // rings, k % rings
+            source = sub_at(order[j], h)
+            target = pl.ds(k * sub, sub)
             users[target, :] = user_ref[source, :]
             pos = pos_col[source, :]
             row = row_col[source, :]
             for t in range(tiles):
                 here = slice(t * LANES, (t + 1) * LANES)
                 value = row_exp[source, here] * row + col_exp[source, here] * col_scale[t : t + 1, :]
-                match = pos == strip_lane + float(t * LANES)
+                match = pos == sub_lane + float(t * LANES)
                 value = value - jnp.where(match, 2.0, 0.0)
                 at = (t % half_tiles) * LANES
                 coupling[t // half_tiles, target, at : at + LANES] = value.astype(jnp.bfloat16)
@@ -264,89 +268,89 @@
         )
 
     leaving = {}
-    hub_half = pl.ds(len(covers) * strip, strip // 2)
-    for index, sign in enumerate(signs):
-        for slot, c in enumerate(covers):
-            leaving.setdefault(-sign * (hub + c) % rings, []).append(
+    hub_half = pl.ds(len(covers) * sub, sub // 2)
+    for h in range(PARTS):
+        for index, sign in enumerate(signs):
+            for slot, c in enumerate(covers):
+                leaving.setdefault((h, -sign * (hub + c) % rings), []).append(
+                    (
+                        part.at[part_at(-sign * (hub + c), h), :],
+                        hub_in.at[h, index, pl.ds(slot * sub, sub), :],
+                        w_sems.at[0],
+                        h_sems.at[h, index],
+                        z_at(-sign * c),
+                    )
+                )
+            first = part_at(rings // 2, h).start + index * (sub // 2)
+            leaving.setdefault((h, rings // 2), []).append(
                 (
-                    part.at[part_at(-sign * (hub + c)), :],
-                    hub_in.at[index, pl.ds(slot * strip, strip), :],
+                    part.at[pl.ds(first, sub // 2), :],
+                    hub_in.at[h, index, hub_half, :],
                     w_sems.at[0],
-                    w_sems.at[1 + index],
-                    z_at(-sign * c),
+                    h_sems.at[h, index],
+                    z_at(-sign * far),
                 )
             )
-        leaving.setdefault(rings // 2, []).append(
-            (
-                part.at[pl.ds(part_at(rings // 2).start + index * (strip // 2), strip // 2), :],
-                hub_in.at[index, hub_half, :],
-                w_sems.at[0],
-                w_sems.at[1 + index],
-                z_at(-sign * far),
-            )
-        )
-        for step in range(1, direct + 1):
-            leaving.setdefault(-sign * step % rings, []).append(
-                (
-                    part.at[part_at(-sign * step), :],
-                    near_in.at[index * direct + step - 1],
-                    w_sems.at[3],
-                    w_sems.at[4],
-                    z_at(-sign * step),
+            for step in range(1, direct + 1):
+                leaving.setdefault((h, -sign * step % rings), []).append(
+                    (
+                        part.at[part_at(-sign * step, h), :],
+                        near_in.at[h, index * direct + step - 1],
+                        w_sems.at[1],
+                        n_sems.at[h],
+                        z_at(-sign * step),
+                    )
                 )
-            )
 
     for b in range(blocks):
         user_block(b)
-        for j in range(b * per_block, (b + 1) * per_block):
-            for copy in leaving.get(order[j], ()):
+        for k in range(b * per_block, (b + 1) * per_block):
+            for copy in leaving.get((k // rings, order[k % rings]), ()):
                 remote(*copy).start()
 
-    def hub_sum(index):
-        sign = signs[index]
-        wait_bytes(hub_in.at[index], w_sems.at[1 + index])
-        span = part_at(-sign * hub)
-        total = part[span, :]
-        for slot in range(len(covers)):
-            total = total + hub_in[index, slot * strip : (slot + 1) * strip, :]
-        part[span, :] = total
-        half = pl.ds(span.start + index * (strip // 2), strip // 2)
-        part[half, :] += hub_in[index, hub_half, :]
-        remote(
-            part.at[span, :],
-            near_in.at[2 * direct + index],
-            w_sems.at[3],
-            w_sems.at[4],
-            z_at(-sign * hub),
-        ).start()
-
-    def own_sum():
-        wait_bytes(near_in, w_sems.at[4])
-        total = part[part_at(0), :]
+    def hub_sum(h):
+        for index, sign in enumerate(signs):
+            wait_bytes(hub_in.at[h, index], h_sems.at[h, index])
+            span = part_at(-sign * hub, h)
+            total = part[span, :]
+            for slot in range(len(covers)):
+                total = total + hub_in[h, index, slot * sub : (slot + 1) * sub, :]
+            part[span, :] = total
+            half = pl.ds(span.start + index * (sub // 2), sub // 2)
+            part[half, :] += hub_in[h, index, hub_half, :]
+            remote(
+                part.at[span, :],
+                near_in.at[h, 2 * direct + index],
+                w_sems.at[1],
+                n_sems.at[h],
+                z_at(-sign * hub),
+            ).start()
+
+    def own_sum(h):
+        wait_bytes(near_in.at[h], n_sems.at[h])
+        total = part[part_at(0, h), :]
         for slot in range(2 * direct + 2):
-            total = total + near_in[slot]
-        span = strip_at(0)
+            total = total + near_in[h, slot]
+        span = sub_at(0, h)
         ug_ref[span, :] = total
         here = ug_ref.at[span, :]
         for index, sign in enumerate(signs):
-            remote(here, here, w_sems.at[5], g_sems.at[index], z_at(sign * hub)).start()
+            remote(here, here, w_sems.at[2], g_sems.at[h, index], z_at(sign * hub)).start()
         for step in range(1, direct + 1):
             for sign in signs:
-                remote(here, here, w_sems.at[5], w_sems.at[6], z_at(sign * step)).start()
-
-    def hub_spread(index):
-        sign = signs[index]
-        start = (ring - sign * hub + rings) % rings * strip
-        here = ug_ref.at[pl.ds(pl.multiple_of(start, strip), strip), :]
-        wait_bytes(here, g_sems.at[index])
-        half_start = pl.multiple_of(start + index * (strip // 2), strip // 2)
-        half = ug_ref.at[pl.ds(half_start, strip // 2), :]
-        remote(half, half, w_sems.at[5], w_sems.at[6], z_at(sign * far)).start()
-        for c in sorted(covers, key=lambda c: -abs(c)):
-            remote(here, here, w_sems.at[5], w_sems.at[6], z_at(sign * c)).start()
+                remote(here, here, w_sems.at[2], w_sems.at[3], z_at(sign * step)).start()
+
+    def hub_spread(h):
+        for index, sign in enumerate(signs):
+            here = ug_ref.at[sub_at(-sign * hub, h), :]
+            wait_bytes(here, g_sems.at[h, index])
+            half = ug_ref.at[sub_at(-sign * hub, h, index * (sub // 2), sub // 2), :]
+            remote(half, half, w_sems.at[2], w_sems.at[3], z_at(sign * far)).start()
+            for c in sorted(covers, key=lambda c: -abs(c)):
+                remote(here, here, w_sems.at[2], w_sems.at[3], z_at(sign * c)).start()
 
     def gather_end():
-        wait_bytes(ug_ref.at[pl.ds(0, (rings - 3) * strip), :], w_sems.at[6])
+        wait_bytes(ug_ref.at[pl.ds(0, (rings - 3) * strip), :], w_sems.at[3])
 
     def item_part(which):
         items[which, :half_cols, :] = 2.0 * lax.dot_general(
@@ -375,13 +379,11 @@
 
     def plane_send():
         wait_bytes(core_in, x_sems.at[1])
-        pair_loss = core_in[half_cols:, :LANES] + loss_rows
+        p_loss[chip] = core_in[half_cols:, :LANES] + loss_rows
 
         def pack(k, carry):
             span = pl.ds(pl.multiple_of(k * piece, piece), piece)
-            plane_out[k, :piece, :] = items[core, span, :] + core_in[span, :]
-            plane_out[k, piece:, :LANES] = pair_loss
-            plane_out[k, piece:, LANES:] = jnp.zeros((8, width - LANES), F32)
+            plane_out[k] = items[core, span, :] + core_in[span, :]
             return carry
 
         lax.fori_loop(0, chips, pack, 0)
@@ -395,6 +397,19 @@
             ).start()
         plane_in[chip] = plane_out[chip]
 
+    def pair_loss_send():
+        for step in chip_steps:
+            remote(
+                p_loss.at[chip], p_loss.at[chip], l_sems.at[2], l_sems.at[3], chip_peer(step)
+            ).start()
+
+    def pair_loss_sum():
+        wait_bytes(p_loss.at[pl.ds(0, chips - 1)], l_sems.at[3])
+        total = p_loss[0]
+        for k in range(1, chips):
+            total = total + p_loss[k]
+        return total
+
     def piece_at(half_index, index):
         start = half_index * half_cols + index % chips * piece
         return pl.ds(pl.multiple_of(start, piece), piece)
@@ -405,20 +420,19 @@
         for k in range(1, chips):
             total = total + plane_in[k]
         here = ig_ref.at[piece_at(core, chip), :]
-        here[...] = total[:piece, :]
+        here[...] = total
         for step in chip_steps:
             remote(
                 here, here, x_sems.at[4], back_sems.at[step - 1], chip_peer(step)
             ).start()
         remote(here, here, x_sems.at[5], x_sems.at[6], (twin, ring)).start()
-        z_loss[ring] = jnp.broadcast_to(
-            item_loss - total[piece + 1 : piece + 2, :LANES], (8, LANES)
-        )
+
+    def loss_send(total):
+        z_loss[ring] = jnp.broadcast_to(item_loss - total[1:2, :], (8, LANES))
         for step in z_steps:
             remote(
                 z_loss.at[ring], z_loss.at[ring], l_sems.at[0], l_sems.at[1], z_peer(step)
             ).start()
-        return total[piece : piece + 1, :LANES]
 
     def forward(step):
         here = ig_ref.at[piece_at(core, chip + chips - step), :]
@@ -436,16 +450,21 @@
 
     core_send()
     item_part(core)
+    hub_sum(0)
     plane_send()
-    hub_sum(0)
     hub_sum(1)
-    own_sum()
-    users_total = plane_sum()
+    own_sum(0)
+    pair_loss_send()
+    own_sum(1)
+    plane_sum()
     hub_spread(0)
     hub_spread(1)
+    plane_total = pair_loss_sum()
+    loss_send(plane_total)
     for step in chip_steps:
         forward(step)
-    loss_end(users_total)
+    loss_end(plane_total[0:1, :])
+
     def half_out(which):
         span = pl.ds(pl.multiple_of(which * half_cols, half_cols), half_cols)
         return pltpu.make_async_copy(ig_ref.at[span, :], ig_hbm.at[span, :], out_sems.at[which])
@@ -461,8 +480,9 @@
     wait_bytes(p_stats.at[pl.ds(0, 2 * chips - 1)], p_sems.at[0])
     wait_bytes(z_loss.at[pl.ds(0, rings - 1)], l_sems.at[0])
     wait_bytes(hub_in, w_sems.at[0])
-    wait_bytes(near_in, w_sems.at[3])
-    wait_bytes(ug_ref.at[pl.ds(0, (rings - 1) * strip), :], w_sems.at[5])
+    wait_bytes(near_in, w_sems.at[1])
+    wait_bytes(ug_ref.at[pl.ds(0, (rings - 1) * strip), :], w_sems.at[2])
+    wait_bytes(p_loss.at[pl.ds(0, chips - 1)], l_sems.at[2])
     wait_bytes(core_in, x_sems.at[0])
     wait_bytes(plane_in.at[pl.ds(0, chips - 1)], x_sems.at[2])
     wait_bytes(ig_ref.at[others, :], x_sems.at[4])
@@ -504,7 +524,8 @@
     tiles = cols // LANES
     strip = rows // rings
     direct = rings // 8
-    hub_rows = (2 * direct if rings > 8 else 1) * strip + strip // 2
+    sub = strip // PARTS
+    hub_rows = (2 * direct if rings > 8 else 1) * sub + sub // 2
     piece = cols // 2 // chips
     vmem = pl.BlockSpec(memory_space=pltpu.VMEM)
     hbm = pl.BlockSpec(memory_space=pltpu.HBM)
@@ -540,16 +561,19 @@
             pltpu.VMEM((rings, rows // LANES, LANES), F32),
             pltpu.VMEM((2 * chips, 2 * tiles, LANES), F32),
             pltpu.VMEM((rings, 8, LANES), F32),
-            pltpu.VMEM((2, hub_rows, width), F32),
-            pltpu.VMEM((2 * direct + 2, strip, width), F32),
+            pltpu.VMEM((PARTS, 2, hub_rows, width), F32),
+            pltpu.VMEM((PARTS, 2 * direct + 2, sub, width), F32),
             pltpu.VMEM((cols // 2 + 8, width), F32),
-            pltpu.VMEM((chips, piece + 8, width), F32),
-            pltpu.VMEM((chips, piece + 8, width), F32),
+            pltpu.VMEM((chips, piece, width), F32),
+            pltpu.VMEM((chips, piece, width), F32),
+            pltpu.VMEM((chips, 8, LANES), F32),
             dma((2,)),
             dma((2,)),
-            dma((2,)),
-            dma((7,)),
-            dma((2,)),
+            dma((4,)),
+            dma((4,)),
+            dma((PARTS, 2)),
+            dma((PARTS,)),
+            dma((PARTS, 2)),
             dma((8,)),
             dma((chips - 1,)),
             dma((2,)),

time: 58.9 us -> 61.4 us (1.042)
  the two profiles are of different devices: /device:TPU:1 before, /device:TPU:8 now
where the time goes in v6:
time: 61.4 us; the launch traced here: 61.1 us
  Pallas kernels  58.7 us (96%)
  between operations  2.41 us (4%)
    pallas_call x1, Pallas kernels, per_device(): pl.pallas_call(functools.partial(kernel, total_users, chips, rings), out_...  56.5 us
    pallas_call x1, Pallas kernels, per_device(): pl.pallas_call(copy_out, out_shape=(jax.ShapeDtypeStruct((rows, width), F...  2.19 us

profile of v6, /device:TPU:8, one launch (start us, length us, event | category | flops | bytes accessed | tf_op | source)
XLA Modules:
  0.0 61.1 jit_solution(8274097046763984110)
XLA Ops:
  0.6 56.5 %two_sided.1 = (f32[512,256]{1,0:T(8,128)}, f32[1024,256]{1,0:T(8,128)}, f32[1,1]{1,0:T(1,128)}) custom-call(bf16[512,256]{1,0:T(8,128)(2,1)} %user_hbm.1, bf16[1024,256]{1,0:T(8,128)(2,1)} %item_hbm.1, s32[4,128]{1,0:T(4,128)} %bitcast.5, s32[4,128]{1,0:T(4,128)} %bitcast.6, s32[8,128]{1,0:T(8,128)} %bitcast.4), custom_call_target="tpu_custom_call" | custom-call | tf_op jit(solution)/shard_map/two_sided/pallas_call | solution.py:533
  57.2 2.2 %copy_out.1 = (f32[512,256]{1,0:T(8,128)}, f32[1024,256]{1,0:T(8,128)}) custom-call(f32[512,256]{1,0:T(8,128)} %get-tuple-element.8.ug_in, f32[1024,256]{1,0:T(8,128)} %get-tuple-element.9.ig_in), custom_call_target="tpu_custom_call" | custom-call | tf_op jit(solution)/shard_map/copy_out/pallas_call | solution.py:593

commit v7 on v5

--- a/solution.py
+++ b/solution.py
@@ -60,6 +60,7 @@
     z_stats,
     p_stats,
     z_loss,
+    z_match,
     hub_in,
     near_in,
     core_in,
@@ -92,18 +93,26 @@
     mine = lax.axis_index("row")
     ring = lax.axis_index("col")
     chip = mine // 2
-    core = mine % 2
+    core = mine - 2 * chip
     other = 1 - core
     twin = chip * 2 + other
 
+    def around(start, size):
+        places = [start + step for step in range(size)]
+        return [jnp.where(place >= size, place - size, place) for place in places]
+
+    rings_from = around(ring, rings)
+    chips_from = around(chip, chips)
+    rows_from = around(mine, 2 * chips)
+
     def z_peer(step):
-        return (mine, (ring + step) % rings)
+        return (mine, rings_from[step])
 
     def chip_peer(step):
-        return (((chip + step) % chips) * 2 + core, ring)
+        return (chips_from[step] * 2 + core, ring)
 
     def row_peer(step):
-        return ((mine + step) % (2 * chips), ring)
+        return (rows_from[step], ring)
 
     z_steps = sorted(range(1, rings), key=lambda k: -min(k, rings - k))
     chip_steps = list(range(1, chips))
@@ -203,14 +212,17 @@
         remote(
             p_stats.at[mine], p_stats.at[mine], p_sems.at[0], p_sems.at[1], row_peer(step)
         ).start()
+    z_match[ring] = jnp.broadcast_to(jnp.sum(z_part, axis=0, keepdims=True), (8, LANES))
+    for step in z_steps:
+        remote(
+            z_match.at[ring], z_match.at[ring], l_sems.at[2], l_sems.at[3], z_peer(step)
+        ).start()
     wait_bytes(z_stats.at[pl.ds(0, rings - 1)], z_sems.at[1])
     row_lse = merged_lse(z_stats[...])
     for k in range(row_tiles):
         span = pl.ds(k * LANES, LANES)
         row_col[span, :] = jnp.exp(row_col[span, :] - columns_of(row_lse[k : k + 1, :]))
     user_loss = jnp.sum(row_lse + log_user, axis=0, keepdims=True)
-    match_loss = jnp.sum(z_part, axis=0, keepdims=True)
-    loss_rows = jnp.concatenate([user_loss, match_loss, jnp.zeros((6, LANES), F32)], axis=0)
     wait_bytes(p_stats.at[pl.ds(0, 2 * chips - 1)], p_sems.at[1])
     item_stats = p_stats[...]
     col_lse = merged_lse(item_stats[:, :tiles])
@@ -229,8 +241,7 @@
     signs = (1, -1)
 
     def strip_at(offset):
-        start = (ring + offset + rings) % rings * strip
-        return pl.ds(pl.multiple_of(start, strip), strip)
+        return pl.ds(pl.multiple_of(rings_from[offset % rings] * strip, strip), strip)
 
     def part_at(offset):
         return pl.ds(order.index(offset % rings) * strip, strip)
@@ -336,7 +347,7 @@
 
     def hub_spread(index):
         sign = signs[index]
-        start = (ring - sign * hub + rings) % rings * strip
+        start = rings_from[-sign * hub % rings] * strip
         here = ug_ref.at[pl.ds(pl.multiple_of(start, strip), strip), :]
         wait_bytes(here, g_sems.at[index])
         half_start = pl.multiple_of(start + index * (strip // 2), strip // 2)
@@ -358,9 +369,23 @@
 
     core_rows = half_cols // CORE_PARTS
 
+    def loss_send():
+        z_loss[ring] = jnp.broadcast_to(item_loss, (8, LANES))
+        for step in z_steps:
+            remote(
+                z_loss.at[ring], z_loss.at[ring], l_sems.at[0], l_sems.at[1], z_peer(step)
+            ).start()
+
+    def loss_rows():
+        total = z_match[0]
+        for k in range(1, rings):
+            total = total + z_match[k]
+        return user_loss - total
+
     def core_send():
         item_part(other)
-        items[other, half_cols:, :LANES] = loss_rows
+        wait_bytes(z_match.at[pl.ds(0, rings - 1)], l_sems.at[3])
+        items[other, half_cols:, :LANES] = loss_rows()
         items[other, half_cols:, LANES:] = jnp.zeros((8, width - LANES), F32)
         for k in range(CORE_PARTS):
             extra = 8 if k == CORE_PARTS - 1 else 0
@@ -375,7 +400,7 @@
 
     def plane_send():
         wait_bytes(core_in, x_sems.at[1])
-        pair_loss = core_in[half_cols:, :LANES] + loss_rows
+        pair_loss = core_in[half_cols:, :LANES] + loss_rows()
 
         def pack(k, carry):
             span = pl.ds(pl.multiple_of(k * piece, piece), piece)
@@ -387,7 +412,7 @@
         lax.fori_loop(0, chips, pack, 0)
         for step in chip_steps:
             remote(
-                plane_out.at[(chip + step) % chips],
+                plane_out.at[chips_from[step]],
                 plane_in.at[chip],
                 x_sems.at[2],
                 x_sems.at[3],
@@ -396,7 +421,7 @@
         plane_in[chip] = plane_out[chip]
 
     def piece_at(half_index, index):
-        start = half_index * half_cols + index % chips * piece
+        start = half_index * half_cols + index * piece
         return pl.ds(pl.multiple_of(start, piece), piece)
 
     def plane_sum():
@@ -411,17 +436,10 @@
                 here, here, x_sems.at[4], back_sems.at[step - 1], chip_peer(step)
             ).start()
         remote(here, here, x_sems.at[5], x_sems.at[6], (twin, ring)).start()
-        z_loss[ring] = jnp.broadcast_to(
-            item_loss - total[piece + 1 : piece + 2, :LANES], (8, LANES)
-        )
-        for step in z_steps:
-            remote(
-                z_loss.at[ring], z_loss.at[ring], l_sems.at[0], l_sems.at[1], z_peer(step)
-            ).start()
-        return total[piece : piece + 1, :LANES]
+        return total[piece : piece + 8, :LANES]
 
     def forward(step):
-        here = ig_ref.at[piece_at(core, chip + chips - step), :]
+        here = ig_ref.at[piece_at(core, chips_from[chips - step]), :]
         wait_bytes(here, back_sems.at[step - 1])
         remote(here, here, x_sems.at[5], x_sems.at[6], (twin, ring)).start()
 
@@ -436,16 +454,17 @@
 
     core_send()
     item_part(core)
-    plane_send()
+    loss_send()
     hub_sum(0)
     hub_sum(1)
+    plane_send()
     own_sum()
-    users_total = plane_sum()
+    plane_total = plane_sum()
     hub_spread(0)
     hub_spread(1)
     for step in chip_steps:
         forward(step)
-    loss_end(users_total)
+    loss_end(plane_total[0:1, :])
     def half_out(which):
         span = pl.ds(pl.multiple_of(which * half_cols, half_cols), half_cols)
         return pltpu.make_async_copy(ig_ref.at[span, :], ig_hbm.at[span, :], out_sems.at[which])
@@ -460,6 +479,7 @@
     wait_bytes(z_stats.at[pl.ds(0, rings - 1)], z_sems.at[0])
     wait_bytes(p_stats.at[pl.ds(0, 2 * chips - 1)], p_sems.at[0])
     wait_bytes(z_loss.at[pl.ds(0, rings - 1)], l_sems.at[0])
+    wait_bytes(z_match.at[pl.ds(0, rings - 1)], l_sems.at[2])
     wait_bytes(hub_in, w_sems.at[0])
     wait_bytes(near_in, w_sems.at[3])
     wait_bytes(ug_ref.at[pl.ds(0, (rings - 1) * strip), :], w_sems.at[5])
@@ -540,6 +560,7 @@
             pltpu.VMEM((rings, rows // LANES, LANES), F32),
             pltpu.VMEM((2 * chips, 2 * tiles, LANES), F32),
             pltpu.VMEM((rings, 8, LANES), F32),
+            pltpu.VMEM((rings, 8, LANES), F32),
             pltpu.VMEM((2, hub_rows, width), F32),
             pltpu.VMEM((2 * direct + 2, strip, width), F32),
             pltpu.VMEM((cols // 2 + 8, width), F32),
@@ -547,7 +568,7 @@
             pltpu.VMEM((chips, piece + 8, width), F32),
             dma((2,)),
             dma((2,)),
-            dma((2,)),
+            dma((4,)),
             dma((7,)),
             dma((2,)),
             dma((8,)),

time: 58.9 us -> 60.7 us (1.031); the launches traced: 58.7 us -> 59.5 us
  Pallas kernels: 56.3 us -> 57.1 us
    pallas_call x1, Pallas kernels: 54.1 us -> 54.9 us  [per_device(): pl.pallas_call(functools.partial(kernel, total_users, chips, rings), out_...]
where the time goes in v7:
time: 60.7 us; the launch traced here: 59.5 us
  Pallas kernels  57.1 us (94%)
  between operations  2.41 us (4%)
    pallas_call x1, Pallas kernels, per_device(): pl.pallas_call(functools.partial(kernel, total_users, chips, rings), out_...  54.9 us
    pallas_call x1, Pallas kernels, per_device(): pl.pallas_call(copy_out, out_shape=(jax.ShapeDtypeStruct((rows, width), F...  2.19 us

profile of v7, /device:TPU:1, one launch (start us, length us, event | category | flops | bytes accessed | tf_op | source)
XLA Modules:
  0.0 59.5 jit_solution(16436085742118094339)
XLA Ops:
  0.6 54.9 %two_sided.1 = (f32[512,256]{1,0:T(8,128)}, f32[1024,256]{1,0:T(8,128)}, f32[1,1]{1,0:T(1,128)}) custom-call(bf16[512,256]{1,0:T(8,128)(2,1)} %user_hbm.1, bf16[1024,256]{1,0:T(8,128)(2,1)} %item_hbm.1, s32[4,128]{1,0:T(4,128)} %bitcast.5, s32[4,128]{1,0:T(4,128)} %bitcast.6, s32[8,128]{1,0:T(8,128)} %bitcast.4), custom_call_target="tpu_custom_call" | custom-call | tf_op jit(solution)/shard_map/two_sided/pallas_call | solution.py:532
  55.6 2.2 %copy_out.1 = (f32[512,256]{1,0:T(8,128)}, f32[1024,256]{1,0:T(8,128)}) custom-call(f32[512,256]{1,0:T(8,128)} %get-tuple-element.8.ug_in, f32[1024,256]{1,0:T(8,128)} %get-tuple-element.9.ig_in), custom_call_target="tpu_custom_call" | custom-call | tf_op jit(solution)/shard_map/copy_out/pallas_call | solution.py:590

commit v8 on v5

--- a/solution.py
+++ b/solution.py
@@ -10,6 +10,7 @@
 MESH = pl.DeviceIdType.MESH
 LANES = 128
 BLOCK = 128
+GROUP = 64
 CORE_PARTS = 4
 F32 = jnp.float32
 
@@ -54,6 +55,7 @@
     lu_col,
     pos_col,
     row_col,
+    row_lse_col,
     col_max,
     col_sum,
     hits_acc,
@@ -135,57 +137,60 @@
         span = pl.ds(k * LANES, LANES)
         lu_col[span, :] = columns_of(log_user[k : k + 1, :])
         pos_col[span, :] = columns_of(local_pos[k : k + 1, :])
-    col_max[...] = jnp.full(col_max.shape, -jnp.inf, F32)
-    col_sum[...] = jnp.zeros(col_sum.shape, F32)
-    hits_acc[...] = jnp.zeros(hits_acc.shape, F32)
     lane = lax.broadcasted_iota(jnp.int32, (BLOCK, LANES), 1).astype(F32)
 
-    def sweep_one(b, z_part):
-        span = pl.ds(pl.multiple_of(b * BLOCK, BLOCK), BLOCK)
-        scores[span, :] = 2.0 * lax.dot_general(
-            user_ref[span, :],
-            item_ref[...],
+    groups = [pl.ds(g * GROUP, GROUP) for g in range(rows_here // GROUP)]
+    group_lane = lane[:GROUP, :]
+
+    item_in.wait()
+    user_in.wait()
+    z_part = jnp.zeros((8, LANES), F32)
+    for n in range(cols_here // width):
+        scores[:, n * width : (n + 1) * width] = 2.0 * lax.dot_general(
+            user_ref[...],
+            item_ref[n * width : (n + 1) * width, :],
             (((1,), (1,)), ((), ())),
             preferred_element_type=F32,
         )
-        lu = lu_col[span, :]
-        pos = pos_col[span, :]
-        top = None
+        for t in range(n * width // LANES, (n + 1) * width // LANES):
+            here = slice(t * LANES, (t + 1) * LANES)
+            tops = None
+            hits = None
+            for span in groups:
+                s = scores[span, here]
+                shifted = s - log_item[t : t + 1, :]
+                row_col[span, :] = shifted if t == 0 else jnp.maximum(row_col[span, :], shifted)
+                top = jnp.max(fold(s - lu_col[span, :]), axis=0)
+                tops = top if tops is None else jnp.maximum(tops, top)
+                match = pos_col[span, :] == group_lane + float(t * LANES)
+                hit = jnp.sum(fold(jnp.where(match, 1.0, 0.0)), axis=0)
+                hits = hit if hits is None else hits + hit
+                z_part = z_part + jnp.sum(fold(jnp.where(match, s + shifted, 0.0)), axis=0)
+            hits_acc[t] = hits
+            top = jnp.broadcast_to(jnp.max(tops, axis=0, keepdims=True), (8, LANES))
+            col_max[t] = top
+            total = jnp.zeros((8, LANES), F32)
+            for span in groups:
+                col = jnp.exp(scores[span, here] - lu_col[span, :] - top[0:1, :])
+                col_exp[span, here] = col
+                total = total + jnp.sum(fold(col), axis=0)
+            col_sum[t] = total
+
+    for span in groups:
+        row_max = jnp.max(row_col[span, :], axis=1, keepdims=True)
+        row_max = jnp.broadcast_to(row_max, (GROUP, LANES))
+        row_col[span, :] = row_max
+        total = jnp.zeros((GROUP, LANES), F32)
         for t in range(tiles):
-            s = scores[span, t * LANES : (t + 1) * LANES]
-            shifted = s - log_item[t : t + 1, :]
-            top = shifted if top is None else jnp.maximum(top, shifted)
-            col_max[t] = jnp.maximum(col_max[t], jnp.max(fold(s - lu), axis=0))
-            match = pos == lane + float(t * LANES)
-            hits_acc[t] += jnp.sum(fold(jnp.where(match, 1.0, 0.0)), axis=0)
-            z_part = z_part + jnp.sum(fold(jnp.where(match, s + shifted, 0.0)), axis=0)
-        row_col[span, :] = jnp.broadcast_to(jnp.max(top, axis=1, keepdims=True), (BLOCK, LANES))
-        return z_part
-
-    item_in.wait()
-    user_in.wait()
-    z_part = lax.fori_loop(0, blocks, sweep_one, jnp.zeros((8, LANES), F32))
-    for t in range(tiles):
-        col_max[t] = jnp.broadcast_to(jnp.max(col_max[t], axis=0, keepdims=True), (8, LANES))
-
-    def sweep_two(b, carry):
-        span = pl.ds(pl.multiple_of(b * BLOCK, BLOCK), BLOCK)
-        lu = lu_col[span, :]
-        row_max = row_col[span, :]
-        total = jnp.zeros((BLOCK, LANES), F32)
-        for t in range(tiles):
-            s = scores[span, t * LANES : (t + 1) * LANES]
-            row = jnp.exp(s - log_item[t : t + 1, :] - row_max)
-            row_exp[span, t * LANES : (t + 1) * LANES] = row
+            here = slice(t * LANES, (t + 1) * LANES)
+            row = jnp.exp(scores[span, here] - log_item[t : t + 1, :] - row_max)
+            row_exp[span, here] = row
             total = total + row
-            col = jnp.exp(s - lu - col_max[t, 0:1, :])
-            col_exp[span, t * LANES : (t + 1) * LANES] = col
-            col_sum[t] += jnp.sum(fold(col), axis=0)
         lse = row_max + jnp.log(jnp.sum(total, axis=1, keepdims=True))
-        z_stats[ring, pl.ds(b, 1), :] = jnp.transpose(lse)[0:1, :]
-        return carry
-
-    lax.fori_loop(0, blocks, sweep_two, 0)
+        row_lse_col[span, :] = lse
+    for k in range(row_tiles):
+        block = row_lse_col[pl.ds(k * LANES, LANES), :]
+        z_stats[ring, k : k + 1, :] = jnp.transpose(block)[0:1, :]
     col_lse_rows = []
     hits_rows = []
     for t in range(tiles):
@@ -531,6 +536,7 @@
             pltpu.VMEM((rows, width), F32),
             pltpu.VMEM((2, cols // 2 + 8, width), F32),
             pltpu.VMEM((tiles, LANES), F32),
+            pltpu.VMEM((rows, LANES), F32),
             pltpu.VMEM((rows, LANES), F32),
             pltpu.VMEM((rows, LANES), F32),
             pltpu.VMEM((rows, LANES), F32),

time: 58.9 us -> 58.9 us (level)
  no operation moved by 1% of the time
where the time goes in v8:
time: 58.9 us; the launch traced here: 58.7 us
  Pallas kernels  56.3 us (96%)
  between operations  2.41 us (4%)
    pallas_call x1, Pallas kernels, per_device(): pl.pallas_call(functools.partial(kernel, total_users, chips, rings), out_...  54.1 us
    pallas_call x1, Pallas kernels, per_device(): pl.pallas_call(copy_out, out_shape=(jax.ShapeDtypeStruct((rows, width), F...  2.19 us

profile of v8, /device:TPU:1, one launch (start us, length us, event | category | flops | bytes accessed | tf_op | source)
XLA Modules:
  0.0 58.7 jit_solution(6233931826865400391)
XLA Ops:
  0.6 54.1 %two_sided.1 = (f32[512,256]{1,0:T(8,128)}, f32[1024,256]{1,0:T(8,128)}, f32[1,1]{1,0:T(1,128)}) custom-call(bf16[512,256]{1,0:T(8,128)(2,1)} %user_hbm.1, bf16[1024,256]{1,0:T(8,128)(2,1)} %item_hbm.1, s32[4,128]{1,0:T(4,128)} %bitcast.5, s32[4,128]{1,0:T(4,128)} %bitcast.6, s32[8,128]{1,0:T(8,128)} %bitcast.4), custom_call_target="tpu_custom_call" | custom-call | tf_op jit(solution)/shard_map/two_sided/pallas_call | solution.py:517
  54.7 2.2 %copy_out.1 = (f32[512,256]{1,0:T(8,128)}, f32[1024,256]{1,0:T(8,128)}) custom-call(f32[512,256]{1,0:T(8,128)} %get-tuple-element.8.ug_in, f32[1024,256]{1,0:T(8,128)} %get-tuple-element.9.ig_in), custom_call_target="tpu_custom_call" | custom-call | tf_op jit(solution)/shard_map/copy_out/pallas_call | solution.py:575

commit v9 on v6

--- a/solution.py
+++ b/solution.py
@@ -61,12 +61,12 @@
     z_stats,
     p_stats,
     z_loss,
+    z_match,
     hub_in,
     near_in,
     core_in,
     plane_out,
     plane_in,
-    p_loss,
     z_sems,
     p_sems,
     l_sems,
@@ -207,14 +207,17 @@
         remote(
             p_stats.at[mine], p_stats.at[mine], p_sems.at[0], p_sems.at[1], row_peer(step)
         ).start()
+    z_match[ring] = jnp.broadcast_to(jnp.sum(z_part, axis=0, keepdims=True), (8, LANES))
+    for step in z_steps:
+        remote(
+            z_match.at[ring], z_match.at[ring], l_sems.at[2], l_sems.at[3], z_peer(step)
+        ).start()
     wait_bytes(z_stats.at[pl.ds(0, rings - 1)], z_sems.at[1])
     row_lse = merged_lse(z_stats[...])
     for k in range(row_tiles):
         span = pl.ds(k * LANES, LANES)
         row_col[span, :] = jnp.exp(row_col[span, :] - columns_of(row_lse[k : k + 1, :]))
     user_loss = jnp.sum(row_lse + log_user, axis=0, keepdims=True)
-    match_loss = jnp.sum(z_part, axis=0, keepdims=True)
-    loss_rows = jnp.concatenate([user_loss, match_loss, jnp.zeros((6, LANES), F32)], axis=0)
     wait_bytes(p_stats.at[pl.ds(0, 2 * chips - 1)], p_sems.at[1])
     item_stats = p_stats[...]
     col_lse = merged_lse(item_stats[:, :tiles])
@@ -362,9 +365,23 @@
 
     core_rows = half_cols // CORE_PARTS
 
+    def loss_send():
+        z_loss[ring] = jnp.broadcast_to(item_loss, (8, LANES))
+        for step in z_steps:
+            remote(
+                z_loss.at[ring], z_loss.at[ring], l_sems.at[0], l_sems.at[1], z_peer(step)
+            ).start()
+
+    def loss_rows():
+        total = z_match[0]
+        for k in range(1, rings):
+            total = total + z_match[k]
+        return user_loss - total
+
     def core_send():
         item_part(other)
-        items[other, half_cols:, :LANES] = loss_rows
+        wait_bytes(z_match.at[pl.ds(0, rings - 1)], l_sems.at[3])
+        items[other, half_cols:, :LANES] = loss_rows()
         items[other, half_cols:, LANES:] = jnp.zeros((8, width - LANES), F32)
         for k in range(CORE_PARTS):
             extra = 8 if k == CORE_PARTS - 1 else 0
@@ -379,11 +396,13 @@
 
     def plane_send():
         wait_bytes(core_in, x_sems.at[1])
-        p_loss[chip] = core_in[half_cols:, :LANES] + loss_rows
+        pair_loss = core_in[half_cols:, :LANES] + loss_rows()
 
         def pack(k, carry):
             span = pl.ds(pl.multiple_of(k * piece, piece), piece)
-            plane_out[k] = items[core, span, :] + core_in[span, :]
+            plane_out[k, :piece, :] = items[core, span, :] + core_in[span, :]
+            plane_out[k, piece:, :LANES] = pair_loss
+            plane_out[k, piece:, LANES:] = jnp.zeros((8, width - LANES), F32)
             return carry
 
         lax.fori_loop(0, chips, pack, 0)
@@ -397,19 +416,6 @@
             ).start()
         plane_in[chip] = plane_out[chip]
 
-    def pair_loss_send():
-        for step in chip_steps:
-            remote(
-                p_loss.at[chip], p_loss.at[chip], l_sems.at[2], l_sems.at[3], chip_peer(step)
-            ).start()
-
-    def pair_loss_sum():
-        wait_bytes(p_loss.at[pl.ds(0, chips - 1)], l_sems.at[3])
-        total = p_loss[0]
-        for k in range(1, chips):
-            total = total + p_loss[k]
-        return total
-
     def piece_at(half_index, index):
         start = half_index * half_cols + index % chips * piece
         return pl.ds(pl.multiple_of(start, piece), piece)
@@ -420,19 +426,13 @@
         for k in range(1, chips):
             total = total + plane_in[k]
         here = ig_ref.at[piece_at(core, chip), :]
-        here[...] = total
+        here[...] = total[:piece, :]
         for step in chip_steps:
             remote(
                 here, here, x_sems.at[4], back_sems.at[step - 1], chip_peer(step)
             ).start()
         remote(here, here, x_sems.at[5], x_sems.at[6], (twin, ring)).start()
-
-    def loss_send(total):
-        z_loss[ring] = jnp.broadcast_to(item_loss - total[1:2, :], (8, LANES))
-        for step in z_steps:
-            remote(
-                z_loss.at[ring], z_loss.at[ring], l_sems.at[0], l_sems.at[1], z_peer(step)
-            ).start()
+        return total[piece : piece + 8, :LANES]
 
     def forward(step):
         here = ig_ref.at[piece_at(core, chip + chips - step), :]
@@ -450,17 +450,15 @@
 
     core_send()
     item_part(core)
+    loss_send()
     hub_sum(0)
     plane_send()
     hub_sum(1)
     own_sum(0)
-    pair_loss_send()
     own_sum(1)
-    plane_sum()
+    plane_total = plane_sum()
     hub_spread(0)
     hub_spread(1)
-    plane_total = pair_loss_sum()
-    loss_send(plane_total)
     for step in chip_steps:
         forward(step)
     loss_end(plane_total[0:1, :])
@@ -482,7 +480,7 @@
     wait_bytes(hub_in, w_sems.at[0])
     wait_bytes(near_in, w_sems.at[1])
     wait_bytes(ug_ref.at[pl.ds(0, (rings - 1) * strip), :], w_sems.at[2])
-    wait_bytes(p_loss.at[pl.ds(0, chips - 1)], l_sems.at[2])
+    wait_bytes(z_match.at[pl.ds(0, rings - 1)], l_sems.at[2])
     wait_bytes(core_in, x_sems.at[0])
     wait_bytes(plane_in.at[pl.ds(0, chips - 1)], x_sems.at[2])
     wait_bytes(ig_ref.at[others, :], x_sems.at[4])
@@ -561,12 +559,12 @@
             pltpu.VMEM((rings, rows // LANES, LANES), F32),
             pltpu.VMEM((2 * chips, 2 * tiles, LANES), F32),
             pltpu.VMEM((rings, 8, LANES), F32),
+            pltpu.VMEM((rings, 8, LANES), F32),
             pltpu.VMEM((PARTS, 2, hub_rows, width), F32),
             pltpu.VMEM((PARTS, 2 * direct + 2, sub, width), F32),
             pltpu.VMEM((cols // 2 + 8, width), F32),
-            pltpu.VMEM((chips, piece, width), F32),
-            pltpu.VMEM((chips, piece, width), F32),
-            pltpu.VMEM((chips, 8, LANES), F32),
+            pltpu.VMEM((chips, piece + 8, width), F32),
+            pltpu.VMEM((chips, piece + 8, width), F32),
             dma((2,)),
             dma((2,)),
             dma((4,)),

time: 61.4 us -> 59.7 us (0.972)
  the two profiles are of different devices: /device:TPU:8 before, /device:TPU:1 now
where the time goes in v9:
time: 59.7 us; the launch traced here: 59.3 us
  Pallas kernels  56.9 us (95%)
  between operations  2.41 us (4%)
    pallas_call x1, Pallas kernels, per_device(): pl.pallas_call(functools.partial(kernel, total_users, chips, rings), out_...  54.7 us
    pallas_call x1, Pallas kernels, per_device(): pl.pallas_call(copy_out, out_shape=(jax.ShapeDtypeStruct((rows, width), F...  2.19 us

profile of v9, /device:TPU:1, one launch (start us, length us, event | category | flops | bytes accessed | tf_op | source)
XLA Modules:
  0.0 59.3 jit_solution(4210647874451451791)
XLA Ops:
  0.6 54.7 %two_sided.1 = (f32[512,256]{1,0:T(8,128)}, f32[1024,256]{1,0:T(8,128)}, f32[1,1]{1,0:T(1,128)}) custom-call(bf16[512,256]{1,0:T(8,128)(2,1)} %user_hbm.1, bf16[1024,256]{1,0:T(8,128)(2,1)} %item_hbm.1, s32[4,128]{1,0:T(4,128)} %bitcast.5, s32[4,128]{1,0:T(4,128)} %bitcast.6, s32[8,128]{1,0:T(8,128)} %bitcast.4), custom_call_target="tpu_custom_call" | custom-call | tf_op jit(solution)/shard_map/two_sided/pallas_call | solution.py:531
  55.3 2.2 %copy_out.1 = (f32[512,256]{1,0:T(8,128)}, f32[1024,256]{1,0:T(8,128)}) custom-call(f32[512,256]{1,0:T(8,128)} %get-tuple-element.8.ug_in, f32[1024,256]{1,0:T(8,128)} %get-tuple-element.9.ig_in), custom_call_target="tpu_custom_call" | custom-call | tf_op jit(solution)/shard_map/copy_out/pallas_call | solution.py:591

commit v10 on v9

--- a/solution.py
+++ b/solution.py
@@ -61,7 +61,6 @@
     z_stats,
     p_stats,
     z_loss,
-    z_match,
     hub_in,
     near_in,
     core_in,
@@ -207,17 +206,14 @@
         remote(
             p_stats.at[mine], p_stats.at[mine], p_sems.at[0], p_sems.at[1], row_peer(step)
         ).start()
-    z_match[ring] = jnp.broadcast_to(jnp.sum(z_part, axis=0, keepdims=True), (8, LANES))
-    for step in z_steps:
-        remote(
-            z_match.at[ring], z_match.at[ring], l_sems.at[2], l_sems.at[3], z_peer(step)
-        ).start()
     wait_bytes(z_stats.at[pl.ds(0, rings - 1)], z_sems.at[1])
     row_lse = merged_lse(z_stats[...])
     for k in range(row_tiles):
         span = pl.ds(k * LANES, LANES)
         row_col[span, :] = jnp.exp(row_col[span, :] - columns_of(row_lse[k : k + 1, :]))
     user_loss = jnp.sum(row_lse + log_user, axis=0, keepdims=True)
+    match_loss = jnp.sum(z_part, axis=0, keepdims=True)
+    loss_rows = jnp.concatenate([user_loss, match_loss, jnp.zeros((6, LANES), F32)], axis=0)
     wait_bytes(p_stats.at[pl.ds(0, 2 * chips - 1)], p_sems.at[1])
     item_stats = p_stats[...]
     col_lse = merged_lse(item_stats[:, :tiles])
@@ -365,23 +361,9 @@
 
     core_rows = half_cols // CORE_PARTS
 
-    def loss_send():
-        z_loss[ring] = jnp.broadcast_to(item_loss, (8, LANES))
-        for step in z_steps:
-            remote(
-                z_loss.at[ring], z_loss.at[ring], l_sems.at[0], l_sems.at[1], z_peer(step)
-            ).start()
-
-    def loss_rows():
-        total = z_match[0]
-        for k in range(1, rings):
-            total = total + z_match[k]
-        return user_loss - total
-
     def core_send():
         item_part(other)
-        wait_bytes(z_match.at[pl.ds(0, rings - 1)], l_sems.at[3])
-        items[other, half_cols:, :LANES] = loss_rows()
+        items[other, half_cols:, :LANES] = loss_rows
         items[other, half_cols:, LANES:] = jnp.zeros((8, width - LANES), F32)
         for k in range(CORE_PARTS):
             extra = 8 if k == CORE_PARTS - 1 else 0
@@ -396,7 +378,7 @@
 
     def plane_send():
         wait_bytes(core_in, x_sems.at[1])
-        pair_loss = core_in[half_cols:, :LANES] + loss_rows()
+        pair_loss = core_in[half_cols:, :LANES] + loss_rows
 
         def pack(k, carry):
             span = pl.ds(pl.multiple_of(k * piece, piece), piece)
@@ -432,7 +414,14 @@
                 here, here, x_sems.at[4], back_sems.at[step - 1], chip_peer(step)
             ).start()
         remote(here, here, x_sems.at[5], x_sems.at[6], (twin, ring)).start()
-        return total[piece : piece + 8, :LANES]
+        z_loss[ring] = jnp.broadcast_to(
+            item_loss - total[piece + 1 : piece + 2, :LANES], (8, LANES)
+        )
+        for step in z_steps:
+            remote(
+                z_loss.at[ring], z_loss.at[ring], l_sems.at[0], l_sems.at[1], z_peer(step)
+            ).start()
+        return total[piece : piece + 1, :LANES]
 
     def forward(step):
         here = ig_ref.at[piece_at(core, chip + chips - step), :]
@@ -450,7 +439,6 @@
 
     core_send()
     item_part(core)
-    loss_send()
     hub_sum(0)
     plane_send()
     hub_sum(1)
@@ -461,7 +449,7 @@
     hub_spread(1)
     for step in chip_steps:
         forward(step)
-    loss_end(plane_total[0:1, :])
+    loss_end(plane_total)
 
     def half_out(which):
         span = pl.ds(pl.multiple_of(which * half_cols, half_cols), half_cols)
@@ -480,7 +468,6 @@
     wait_bytes(hub_in, w_sems.at[0])
     wait_bytes(near_in, w_sems.at[1])
     wait_bytes(ug_ref.at[pl.ds(0, (rings - 1) * strip), :], w_sems.at[2])
-    wait_bytes(z_match.at[pl.ds(0, rings - 1)], l_sems.at[2])
     wait_bytes(core_in, x_sems.at[0])
     wait_bytes(plane_in.at[pl.ds(0, chips - 1)], x_sems.at[2])
     wait_bytes(ig_ref.at[others, :], x_sems.at[4])
@@ -558,7 +545,6 @@
             pltpu.VMEM((tiles, 8, LANES), F32),
             pltpu.VMEM((rings, rows // LANES, LANES), F32),
             pltpu.VMEM((2 * chips, 2 * tiles, LANES), F32),
-            pltpu.VMEM((rings, 8, LANES), F32),
             pltpu.VMEM((rings, 8, LANES), F32),
             pltpu.VMEM((PARTS, 2, hub_rows, width), F32),
             pltpu.VMEM((PARTS, 2 * direct + 2, sub, width), F32),

time: 59.7 us -> 58.7 us (0.983)
  Pallas kernels: 56.9 us -> 56 us
    pallas_call x1, Pallas kernels: 54.7 us -> 53.8 us  [per_device(): pl.pallas_call(functools.partial(kernel, total_users, chips, rings), out_...]
where the time goes in v10:
time: 58.7 us; the launch traced here: 58.4 us
  Pallas kernels  56 us (95%)
  between operations  2.41 us (4%)
    pallas_call x1, Pallas kernels, per_device(): pl.pallas_call(functools.partial(kernel, total_users, chips, rings), out_...  53.8 us
    pallas_call x1, Pallas kernels, per_device(): pl.pallas_call(copy_out, out_shape=(jax.ShapeDtypeStruct((rows, width), F...  2.19 us

profile of v10, /device:TPU:1, one launch (start us, length us, event | category | flops | bytes accessed | tf_op | source)
XLA Modules:
  0.0 58.4 jit_solution(9359565741508955361)
XLA Ops:
  0.6 53.8 %two_sided.1 = (f32[512,256]{1,0:T(8,128)}, f32[1024,256]{1,0:T(8,128)}, f32[1,1]{1,0:T(1,128)}) custom-call(bf16[512,256]{1,0:T(8,128)(2,1)} %user_hbm.1, bf16[1024,256]{1,0:T(8,128)(2,1)} %item_hbm.1, s32[4,128]{1,0:T(4,128)} %bitcast.5, s32[4,128]{1,0:T(4,128)} %bitcast.6, s32[8,128]{1,0:T(8,128)} %bitcast.4), custom_call_target="tpu_custom_call" | custom-call | tf_op jit(solution)/shard_map/two_sided/pallas_call | solution.py:518
  54.4 2.2 %copy_out.1 = (f32[512,256]{1,0:T(8,128)}, f32[1024,256]{1,0:T(8,128)}) custom-call(f32[512,256]{1,0:T(8,128)} %get-tuple-element.8.ug_in, f32[1024,256]{1,0:T(8,128)} %get-tuple-element.9.ig_in), custom_call_target="tpu_custom_call" | custom-call | tf_op jit(solution)/shard_map/copy_out/pallas_call | solution.py:577

commit v11 on v10

--- a/solution.py
+++ b/solution.py
@@ -59,6 +59,7 @@
     col_sum,
     hits_acc,
     z_stats,
+    c_stats,
     p_stats,
     z_loss,
     hub_in,
@@ -67,6 +68,7 @@
     plane_out,
     plane_in,
     z_sems,
+    s_sems,
     p_sems,
     l_sems,
     w_sems,
@@ -105,18 +107,15 @@
     def chip_peer(step):
         return (((chip + step) % chips) * 2 + core, ring)
 
-    def row_peer(step):
-        return ((mine + step) % (2 * chips), ring)
-
     z_steps = sorted(range(1, rings), key=lambda k: -min(k, rings - k))
     chip_steps = list(range(1, chips))
-    row_steps = list(range(1, 2 * chips))
 
     barrier = pltpu.get_barrier_semaphore()
     for step in z_steps:
         pl.semaphore_signal(barrier, inc=1, device_id=z_peer(step), device_id_type=MESH)
-    for step in row_steps:
-        pl.semaphore_signal(barrier, inc=1, device_id=row_peer(step), device_id_type=MESH)
+    for step in chip_steps:
+        pl.semaphore_signal(barrier, inc=1, device_id=chip_peer(step), device_id_type=MESH)
+    pl.semaphore_signal(barrier, inc=1, device_id=(twin, ring), device_id_type=MESH)
 
     def remote(src, dst, send_sem, recv_sem, device):
         return pltpu.make_async_remote_copy(
@@ -195,16 +194,22 @@
         total = jnp.sum(col_sum[t], axis=0, keepdims=True)
         col_lse_rows.append(col_max[t, 0:1, :] + jnp.log(total))
         hits_rows.append(jnp.sum(hits_acc[t], axis=0, keepdims=True))
-    p_stats[mine] = jnp.concatenate(col_lse_rows + hits_rows, axis=0)
-
-    pl.semaphore_wait(barrier, rings - 1 + 2 * chips - 1)
+    c_stats[0] = jnp.concatenate(col_lse_rows + hits_rows, axis=0)
+
+    pl.semaphore_wait(barrier, rings - 1 + chips - 1 + 1)
+    core_stat = remote(c_stats.at[0], c_stats.at[1], s_sems.at[0], s_sems.at[1], (twin, ring))
+    core_stat.start()
     for step in z_steps:
         remote(
             z_stats.at[ring], z_stats.at[ring], z_sems.at[0], z_sems.at[1], z_peer(step)
         ).start()
-    for step in row_steps:
+    core_stat.wait()
+    one, two = c_stats[0], c_stats[1]
+    p_stats[chip, 0:tiles, :] = merged_lse(jnp.stack([one[:tiles], two[:tiles]]))
+    p_stats[chip, tiles : 2 * tiles, :] = one[tiles:] + two[tiles:]
+    for step in chip_steps:
         remote(
-            p_stats.at[mine], p_stats.at[mine], p_sems.at[0], p_sems.at[1], row_peer(step)
+            p_stats.at[chip], p_stats.at[chip], p_sems.at[0], p_sems.at[1], chip_peer(step)
         ).start()
     wait_bytes(z_stats.at[pl.ds(0, rings - 1)], z_sems.at[1])
     row_lse = merged_lse(z_stats[...])
@@ -214,7 +219,7 @@
     user_loss = jnp.sum(row_lse + log_user, axis=0, keepdims=True)
     match_loss = jnp.sum(z_part, axis=0, keepdims=True)
     loss_rows = jnp.concatenate([user_loss, match_loss, jnp.zeros((6, LANES), F32)], axis=0)
-    wait_bytes(p_stats.at[pl.ds(0, 2 * chips - 1)], p_sems.at[1])
+    wait_bytes(p_stats.at[pl.ds(0, chips - 1)], p_sems.at[1])
     item_stats = p_stats[...]
     col_lse = merged_lse(item_stats[:, :tiles])
     pos_hits = jnp.sum(item_stats[:, tiles:], axis=0)
@@ -463,7 +468,7 @@
     half_out(other).start()
 
     wait_bytes(z_stats.at[pl.ds(0, rings - 1)], z_sems.at[0])
-    wait_bytes(p_stats.at[pl.ds(0, 2 * chips - 1)], p_sems.at[0])
+    wait_bytes(p_stats.at[pl.ds(0, chips - 1)], p_sems.at[0])
     wait_bytes(z_loss.at[pl.ds(0, rings - 1)], l_sems.at[0])
     wait_bytes(hub_in, w_sems.at[0])
     wait_bytes(near_in, w_sems.at[1])
@@ -544,13 +549,15 @@
             pltpu.VMEM((tiles, 8, LANES), F32),
             pltpu.VMEM((tiles, 8, LANES), F32),
             pltpu.VMEM((rings, rows // LANES, LANES), F32),
-            pltpu.VMEM((2 * chips, 2 * tiles, LANES), F32),
+            pltpu.VMEM((2, 2 * tiles, LANES), F32),
+            pltpu.VMEM((chips, 2 * tiles, LANES), F32),
             pltpu.VMEM((rings, 8, LANES), F32),
             pltpu.VMEM((PARTS, 2, hub_rows, width), F32),
             pltpu.VMEM((PARTS, 2 * direct + 2, sub, width), F32),
             pltpu.VMEM((cols // 2 + 8, width), F32),
             pltpu.VMEM((chips, piece + 8, width), F32),
             pltpu.VMEM((chips, piece + 8, width), F32),
+            dma((2,)),
             dma((2,)),
             dma((2,)),
             dma((4,)),

time: 58.7 us -> 58 us (0.988)
  Pallas kernels: 56 us -> 55.4 us
where the time goes in v11:
time: 58 us; the launch traced here: 57.8 us
  Pallas kernels  55.4 us (96%)
  between operations  2.41 us (4%)
    pallas_call x1, Pallas kernels, per_device(): pl.pallas_call(functools.partial(kernel, total_users, chips, rings), out_...  53.2 us
    pallas_call x1, Pallas kernels, per_device(): pl.pallas_call(copy_out, out_shape=(jax.ShapeDtypeStruct((rows, width), F...  2.19 us

profile of v11, /device:TPU:1, one launch (start us, length us, event | category | flops | bytes accessed | tf_op | source)
XLA Modules:
  0.0 57.8 jit_solution(18268421236500520908)
XLA Ops:
  0.6 53.2 %two_sided.1 = (f32[512,256]{1,0:T(8,128)}, f32[1024,256]{1,0:T(8,128)}, f32[1,1]{1,0:T(1,128)}) custom-call(bf16[512,256]{1,0:T(8,128)(2,1)} %user_hbm.1, bf16[1024,256]{1,0:T(8,128)(2,1)} %item_hbm.1, s32[4,128]{1,0:T(4,128)} %bitcast.5, s32[4,128]{1,0:T(4,128)} %bitcast.6, s32[8,128]{1,0:T(8,128)} %bitcast.4), custom_call_target="tpu_custom_call" | custom-call | tf_op jit(solution)/shard_map/two_sided/pallas_call | solution.py:523
  53.9 2.2 %copy_out.1 = (f32[512,256]{1,0:T(8,128)}, f32[1024,256]{1,0:T(8,128)}) custom-call(f32[512,256]{1,0:T(8,128)} %get-tuple-element.8.ug_in, f32[1024,256]{1,0:T(8,128)} %get-tuple-element.9.ig_in), custom_call_target="tpu_custom_call" | custom-call | tf_op jit(solution)/shard_map/copy_out/pallas_call | solution.py:584

commit v12 on v11

--- a/solution.py
+++ b/solution.py
@@ -419,14 +419,14 @@
                 here, here, x_sems.at[4], back_sems.at[step - 1], chip_peer(step)
             ).start()
         remote(here, here, x_sems.at[5], x_sems.at[6], (twin, ring)).start()
-        z_loss[ring] = jnp.broadcast_to(
-            item_loss - total[piece + 1 : piece + 2, :LANES], (8, LANES)
-        )
+        return total[piece : piece + 8, :LANES]
+
+    def loss_send(total):
+        z_loss[ring] = jnp.broadcast_to(item_loss - total[1:2, :], (8, LANES))
         for step in z_steps:
             remote(
                 z_loss.at[ring], z_loss.at[ring], l_sems.at[0], l_sems.at[1], z_peer(step)
             ).start()
-        return total[piece : piece + 1, :LANES]
 
     def forward(step):
         here = ig_ref.at[piece_at(core, chip + chips - step), :]
@@ -451,10 +451,11 @@
     own_sum(1)
     plane_total = plane_sum()
     hub_spread(0)
+    loss_send(plane_total)
     hub_spread(1)
     for step in chip_steps:
         forward(step)
-    loss_end(plane_total)
+    loss_end(plane_total[0:1, :])
 
     def half_out(which):
         span = pl.ds(pl.multiple_of(which * half_cols, half_cols), half_cols)

time: 58 us -> 59.6 us (1.028)
  the two profiles are of different devices: /device:TPU:1 before, /device:TPU:8 now
where the time goes in v12:
time: 59.6 us; the launch traced here: 59.4 us
  Pallas kernels  57 us (96%)
  between operations  2.41 us (4%)
    pallas_call x1, Pallas kernels, per_device(): pl.pallas_call(functools.partial(kernel, total_users, chips, rings), out_...  54.8 us
    pallas_call x1, Pallas kernels, per_device(): pl.pallas_call(copy_out, out_shape=(jax.ShapeDtypeStruct((rows, width), F...  2.19 us

profile of v12, /device:TPU:8, one launch (start us, length us, event | category | flops | bytes accessed | tf_op | source)
XLA Modules:
  0.0 59.4 jit_solution(12012594029800919197)
XLA Ops:
  0.6 54.8 %two_sided.1 = (f32[512,256]{1,0:T(8,128)}, f32[1024,256]{1,0:T(8,128)}, f32[1,1]{1,0:T(1,128)}) custom-call(bf16[512,256]{1,0:T(8,128)(2,1)} %user_hbm.1, bf16[1024,256]{1,0:T(8,128)(2,1)} %item_hbm.1, s32[4,128]{1,0:T(4,128)} %bitcast.5, s32[4,128]{1,0:T(4,128)} %bitcast.6, s32[8,128]{1,0:T(8,128)} %bitcast.4), custom_call_target="tpu_custom_call" | custom-call | tf_op jit(solution)/shard_map/two_sided/pallas_call | solution.py:524
  55.4 2.2 %copy_out.1 = (f32[512,256]{1,0:T(8,128)}, f32[1024,256]{1,0:T(8,128)}) custom-call(f32[512,256]{1,0:T(8,128)} %get-tuple-element.8.ug_in, f32[1024,256]{1,0:T(8,128)} %get-tuple-element.9.ig_in), custom_call_target="tpu_custom_call" | custom-call | tf_op jit(solution)/shard_map/copy_out/pallas_call | solution.py:585
